TPU v7x, 32 devices: a whole 2x2x4 slice. The times are simulated.
32 devices in a mesh: dp: 4 (over y, x), ctx: 8 (over z, core).
Axes of the slice: x: 2, y: 2, z: 4, core: 2. Of those that a mesh axis runs over, the one named last changes fastest.
Arguments:
- queries: bfloat16 [4, 1024, 1024], P('dp', 'ctx'), may hold values from -180 to 180
- keys: bfloat16 [4, 4096, 128], P('dp', 'ctx'), may hold values from -6 to 6
- values: bfloat16 [4, 4096, 128], P('dp', 'ctx'), may hold values from -6 to 6
- grad_out: bfloat16 [4, 1024, 1024], P('dp', 'ctx'), may hold values from -6 to 6
- saved_out: bfloat16 [4, 1024, 1024], P('dp', 'ctx'), may hold values from -1.796875 to 1.796875
- segment_ids: int32 [4, 4096], P('dp', 'ctx'), may hold values from 0 to 31, never falling along the last dimension, each value on 1 to 1024 neighbouring positions
- frame_flags: int32 [4, 32], P('dp'), may hold values 0 or 1
Outputs:
- grad_queries: bfloat16 [4, 1024, 1024], P('dp', 'ctx')
- grad_keys: bfloat16 [4, 4096, 128], P('dp', 'ctx')
- grad_values: bfloat16 [4, 4096, 128], P('dp', 'ctx')
All inputs are finite; a program needn't handle non-finite values. No bound on the sum of `frame_flags` on one device may be relied on, other than what follows from the above.
Results may differ from a plain program's by a relative error of at most 0.0051.
Values may be sent and summed in bfloat16 or wider, within the bound.
A program may use at most 64 MiB of HBM per device.

v0:
```python
import math

import jax
import jax.numpy as jnp
from jax import lax
from jax.sharding import PartitionSpec as P

H = 8
HD = 128


def from_behind(value, axis, steps):
    count = lax.axis_size(axis)
    pairs = [(source, (source + steps) % count) for source in range(count)]
    return lax.ppermute(value, axis, pairs)


def split_blocks(row_count):
    block_size = math.gcd(row_count, 512)
    return (block_size, row_count // block_size)


def contract_rows(left, right):
    return lax.dot_general(
        left, right, (((0,), (0,)), ((), ())), preferred_element_type=jnp.float32
    )


def contract_cols(left, right):
    return lax.dot_general(
        left, right, (((1,), (1,)), ((), ())), preferred_element_type=jnp.float32
    )


def per_device(queries, keys, values, grad_out, saved_out, segment_ids, frame_flags):
    key_rows = keys.shape[1]
    query_rows = queries.shape[1]
    head_rows = query_rows * H
    score_scale = 1.0 / math.sqrt(HD)
    rank_count = lax.axis_size("ctx")
    my_rank = lax.axis_index("ctx")
    seg_whole = lax.all_gather(segment_ids, "ctx", axis=1, tiled=True)[0]
    segment_count = frame_flags.shape[1]
    query_seg = segment_ids[0, key_rows - query_rows :]
    onehot = query_seg[:, None] == jnp.arange(segment_count, dtype=jnp.int32)[None, :]
    query_frame = jnp.sum(jnp.where(onehot, frame_flags[0][None, :], 0), axis=1)
    first_pos = my_rank * key_rows + key_rows - query_rows
    row_pos = first_pos + jnp.arange(head_rows, dtype=jnp.int32) // H
    row_seg = jnp.repeat(query_seg, H)
    row_frame = jnp.repeat(query_frame, H) == 1
    query_mat = queries[0].reshape(head_rows, HD)
    grad_mat = grad_out[0].reshape(head_rows, HD)
    out_dot = jnp.sum(
        (grad_out[0].astype(jnp.float32) * saved_out[0].astype(jnp.float32)).reshape(head_rows, HD),
        axis=1,
    )

    def visible_of(first_row, row_count):
        positions = first_row + jnp.arange(row_count, dtype=jnp.int32)
        key_seg = lax.dynamic_slice_in_dim(seg_whole, first_row, row_count)
        causal = positions[None, :] <= row_pos[:, None]
        framed = (key_seg[None, :] == row_seg[:, None]) & row_frame[:, None]
        return causal | framed

    top_start = jnp.full((head_rows,), -1e30, jnp.float32)
    total_start = jnp.zeros((head_rows,), jnp.float32)
    key_piece = lax.all_gather(keys, "ctx", axis=1, tiled=True)
    block_size, number = split_blocks(key_piece.shape[1])

    def stats_one_block(block_index, running):
        row_top, totals = running
        offset = block_index * block_size
        key_block = lax.dynamic_slice_in_dim(key_piece[0], offset, block_size, 0)
        visible = visible_of(offset, block_size)

        def stats_compute_tile():
            scores = jnp.where(visible, contract_cols(query_mat, key_block) * score_scale, -1e30)
            new_top = jnp.maximum(row_top, jnp.max(scores, axis=1))
            weights = jnp.where(visible, jnp.exp(scores - new_top[:, None]), 0.0)
            return (new_top, totals * jnp.exp(row_top - new_top) + jnp.sum(weights, axis=1))

        def stats_skip_tile():
            return (row_top, totals)

        return lax.cond(jnp.any(visible), stats_compute_tile, stats_skip_tile)

    row_top, totals = lax.fori_loop(0, number, stats_one_block, (top_start, total_start))
    log_total = row_top + jnp.log(totals)

    def grads_tile(key_block, value_block, first_row, query_grad):
        row_count = key_block.shape[0]
        visible = visible_of(first_row, row_count)

        def grads_compute_tile():
            probs = jnp.where(
                visible,
                jnp.exp(contract_cols(query_mat, key_block) * score_scale - log_total[:, None]),
                0.0,
            )
            value_part = contract_rows(probs.astype(jnp.bfloat16), grad_mat)
            dprobs = contract_cols(grad_mat, value_block)
            dscores = (probs * (dprobs - out_dot[:, None])).astype(jnp.bfloat16)
            new_grad = query_grad + score_scale * jnp.dot(
                dscores, key_block, preferred_element_type=jnp.float32
            )
            key_part = score_scale * contract_rows(dscores, query_mat)
            return (new_grad, key_part, value_part)

        def grads_skip_tile():
            zeros_block = jnp.zeros((row_count, HD), jnp.float32)
            return (query_grad, zeros_block, zeros_block)

        return lax.cond(jnp.any(visible), grads_compute_tile, grads_skip_tile)

    def grads_shard(key_part, value_part, first_row, query_grad, key_grad, value_grad):
        block_size, number = split_blocks(key_part.shape[0])

        def grads_one_block(block_index, running):
            grad_now, key_now, value_now = running
            offset = block_index * block_size
            grad_now, key_add, value_add = grads_tile(
                key_part, value_part, first_row + offset, grad_now
            )
            key_now = key_now + key_add
            value_now = value_now + value_add
            return (grad_now, key_now, value_now)

        return lax.fori_loop(0, number, grads_one_block, (query_grad, key_grad, value_grad))

    query_start = jnp.zeros((head_rows, HD), jnp.float32)

    def pass_step(pass_index, carried):
        key_now, value_now, key_grad, value_grad, query_grad = carried
        first_row = (my_rank - pass_index) % rank_count * key_rows
        query_grad, key_grad, value_grad = grads_shard(
            key_now, value_now, first_row, query_grad, key_grad, value_grad
        )
        key_now, value_now = from_behind((key_now, value_now), "ctx", 1)
        key_grad, value_grad = from_behind((key_grad, value_grad), "ctx", 1)
        return (key_now, value_now, key_grad, value_grad, query_grad)

    zeros_shard = jnp.zeros((key_rows, HD), jnp.float32)
    carried = lax.fori_loop(
        0, rank_count - 1, pass_step, (keys[0], values[0], zeros_shard, zeros_shard, query_start)
    )
    key_now, value_now, key_grad, value_grad, query_grad = carried
    last_row = (my_rank + 1) % rank_count * key_rows
    query_grad, key_grad, value_grad = grads_shard(
        key_now, value_now, last_row, query_grad, key_grad, value_grad
    )
    key_grad, value_grad = (
        from_behind(key_grad.astype(jnp.bfloat16), "ctx", 1).astype(key_grad.dtype),
        from_behind(value_grad.astype(jnp.bfloat16), "ctx", 1).astype(value_grad.dtype),
    )
    grad_queries = query_grad.astype(jnp.bfloat16).reshape(1, query_rows, H * HD)
    grad_keys = key_grad.astype(jnp.bfloat16)[None]
    grad_values = value_grad.astype(jnp.bfloat16)[None]
    return (grad_queries, grad_keys, grad_values)


def solution(mesh):
    return jax.shard_map(
        per_device,
        mesh=mesh,
        in_specs=(
            P("dp", "ctx", None),
            P("dp", "ctx", None),
            P("dp", "ctx", None),
            P("dp", "ctx", None),
            P("dp", "ctx", None),
            P("dp", "ctx"),
            P("dp", None),
        ),
        out_specs=(P("dp", "ctx", None), P("dp", "ctx", None), P("dp", "ctx", None)),
        check_vma=False,
    )
```

profile of v0, /device:TPU:0, one launch (start us, length us, event | category | flops | bytes accessed | tf_op | source)
XLA Modules:
  0.0 204.9 jit_solution(213233978120691148)
XLA Ops:
  7.2 1.6 copy.64
  12.8 14.5 %all_gather.6 = s32[1,4096]{1,0:T(1,128)S(1)} all-gather(s32[1,512]{1,0:T(1,128)} %param.22), channel_id=1, replica_groups=mesh['dp'=4,'ctx'=8] {'ctx'}, dimensions={1}, use_global_device_ids=true | all-gather | bytes 18432 | tf_op jit(solution)/shard_map/all_gather | solution.py:42
  27.3 2.3 %fusion.37 = (pred[]{:T(512)}, pred[1024,512]{1,0:T(32,128)(4,1)}) fusion(pred[1024]{0:T(1024)(128)(4,1)S(1)} %eq.160, s32[1024]{0:T(1024)S(1)} %eq.153, s32[512]{0:T(512)S(1)} %bitcast.44, s32[1024]{0:T(1024)S(1)} %fusion.31, s32[512]{0:T(512)S(1)} %iota_add_fusion.2), kind=kLoop, calls=%fused_computation.69 | loop fusion | flops 2621439 | bytes 537601 | tf_op jit(solution)/shard_map/while/body/eval_jaxpr/reduce_or | solution.py:113
  30.6 4.4 %all-gather.2.cloned.1.call-done = bf16[1,4096,128]{2,1,0:T(8,128)(2,1)} async-done(((bf16[1,512,128]{2,1,0:T(8,128)(2,1)}), bf16[1,4096,128]{2,1,0:T(8,128)(2,1)}) %all-gather.2.cloned.1.call-update) | async-done | bytes 1048592 | tf_op jit(solution)/shard_map/all_gather | solution.py:67
  35.0 24.7 %while.68 = (s32[]{:T(128)}, f32[1024]{0:T(1024)S(1)}, f32[1024]{0:T(1024)S(1)}, s32[4096]{0:T(1024)S(1)}, bf16[1,4096,128]{2,1,0:T(8,128)(2,1)}, /*index=5*/bf1...) while((s32[]{:T(128)}, f32[1024]{0:T(1024)S(1)}, ...), condition=%wide.region_8.9_spmd.clone, body=%wide.region_2.8_spmd.clone.sunk | while | flops 141045248 | bytes 6253973 | solution.py:87
  37.6 2.1 %conditional.8 = ((f32[1024]{0:T(1024)S(1)}, f32[1024]{0:T(1024)S(1)})) conditional(s32[]{:T(128)} %convert_element_type.87, (f32[1024]{0:T(1024)S(1)}, f32[1024]{0:T(1024)S(1)}) %tuple.122, (bf16[1,4096,128]{2,1,0:T(8,128)(2,1)}, s32[]{:T(128)}, bf16[1024,128]{1,0:T(8,128)(2,1)S(1)}, pred[1024,512]{0,1:T(32,128)(4,1)S(1)}, f32[1024]{0:T(1024)S(1)}, ...), branch_computations={%region_4.4_spmd, %region_5.7_spmd} | conditional | flops 138414080 | bytes 5689880 | solution.py:85
  42.2 2.1 %conditional.8 = ((f32[1024]{0:T(1024)S(1)}, f32[1024]{0:T(1024)S(1)})) conditional(s32[]{:T(128)} %convert_element_type.87, (f32[1024]{0:T(1024)S(1)}, f32[1024]{0:T(1024)S(1)}) %tuple.122, (bf16[1,4096,128]{2,1,0:T(8,128)(2,1)}, s32[]{:T(128)}, bf16[1024,128]{1,0:T(8,128)(2,1)S(1)}, pred[1024,512]{0,1:T(32,128)(4,1)S(1)}, f32[1024]{0:T(1024)S(1)}, ...), branch_computations={%region_4.4_spmd, %region_5.7_spmd} | conditional | flops 138414080 | bytes 5689880 | solution.py:85
  59.8 125.6 %while.69 = (s32[]{:T(128)}, bf16[512,128]{1,0:T(8,128)(2,1)S(1)}, bf16[512,128]{1,0:T(8,128)(2,1)S(1)}, f32[512,128]{1,0:T(8,128)S(1)}, f32[512,128]{1,0:T(8,12...) while((s32[]{:T(128)}, bf16[512,128]{1,0:T(8,128)(2,1)S(1)}, ...), condition=%wide.region_14.15_spmd.clone, body=%wide.region_10.14_spmd.clone.sunk | while | flops 677848576 | bytes 18791660 | solution.py:143
  60.4 1.5 fusion.64
  62.5 2.6 %conditional.9 = (f32[1024,128]{1,0:T(8,128)S(1)}, f32[512,128]{1,0:T(8,128)S(1)}, f32[512,128]{1,0:T(8,128)S(1)}) conditional(s32[]{:T(128)} %convert_element_type.88, f32[1024,128]{1,0:T(8,128)S(1)} %get-tuple-element.1119, (bf16[1024,128]{1,0:T(8,128)(2,1)S(1)}, bf16[512,128]{1,0:T(8,128)(2,1)S(1)}, f32[1024]{0:T(1024)S(1)}, ...), branch_computations={%region_12.12_spmd, %region_13.13_spmd} | conditional | flops 675086336 | bytes 12984344 | solution.py:113
  65.4 3.8 %collective-permute-start.2 = (f32[512,128]{1,0:T(8,128)S(1)}, f32[512,128]{1,0:T(8,128)S(1)}, u32[]{:S(2)}, u32[]{:S(2)}) collective-permute-start(f32[512,128]{1,0:T(8,128)S(1)} %add.288), channel_id=1, source_target_pairs={{0,1},{1,2},{2,3},{3,4},{4,5},{5,6},{6,7},{7,0},{8,9},{9,10},{10,1... | collective-permute-start | bytes 786440 | tf_op jit(solution)/shard_map/while/body/eval_jaxpr/ppermute | solution.py:15
  69.3 4.4 %collective-permute-start = (bf16[512,128]{1,0:T(8,128)(2,1)S(1)}, bf16[512,128]{1,0:T(8,128)(2,1)S(1)}, u32[]{:S(2)}, u32[]{:S(2)}) collective-permute-start(bf16[512,128]{1,0:T(8,128)(2,1)S(1)} %copy.36), channel_id=1, source_target_pairs={{0,1},{1,2},{2,3},{3,4},{4,5},{5,6},{6,7},{7,0},{8,9},{9,10},{10,1... | collective-permute-start | bytes 393224 | tf_op jit(solution)/shard_map/while/body/eval_jaxpr/ppermute | solution.py:15
  73.7 2.9 %collective-permute-start.1 = (bf16[512,128]{1,0:T(8,128)(2,1)S(1)}, bf16[512,128]{1,0:T(8,128)(2,1)S(1)}, u32[]{:S(2)}, u32[]{:S(2)}) collective-permute-start(bf16[512,128]{1,0:T(8,128)(2,1)S(1)} %copy.37), channel_id=1, source_target_pairs={{0,1},{1,2},{2,3},{3,4},{4,5},{5,6},{6,7},{7,0},{8,9},{9,10},{10,1... | collective-permute-start | bytes 393224 | tf_op jit(solution)/shard_map/while/body/eval_jaxpr/ppermute | solution.py:15
  76.6 11.2 %collective-permute-done = bf16[512,128]{1,0:T(8,128)(2,1)S(1)} collective-permute-done((bf16[512,128]{1,0:T(8,128)(2,1)S(1)}, bf16[512,128]{1,0:T(8,128)(2,1)S(1)}, u32[]{:S(2)}, u32[]{:S(2)}) %collective-permute-start) | collective-permute-done | bytes 131104 | tf_op jit(solution)/shard_map/while/body/eval_jaxpr/ppermute | solution.py:15
  89.7 1.5 fusion.64
  93.4 10.5 %collective-permute-done = bf16[512,128]{1,0:T(8,128)(2,1)S(1)} collective-permute-done((bf16[512,128]{1,0:T(8,128)(2,1)S(1)}, bf16[512,128]{1,0:T(8,128)(2,1)S(1)}, u32[]{:S(2)}, u32[]{:S(2)}) %collective-permute-start) | collective-permute-done | bytes 131104 | tf_op jit(solution)/shard_map/while/body/eval_jaxpr/ppermute | solution.py:15
  105.8 1.5 fusion.64
  108.3 1.8 collective-permute-start.1
  110.1 9.8 %collective-permute-done = bf16[512,128]{1,0:T(8,128)(2,1)S(1)} collective-permute-done((bf16[512,128]{1,0:T(8,128)(2,1)S(1)}, bf16[512,128]{1,0:T(8,128)(2,1)S(1)}, u32[]{:S(2)}, u32[]{:S(2)}) %collective-permute-start) | collective-permute-done | bytes 131104 | tf_op jit(solution)/shard_map/while/body/eval_jaxpr/ppermute | solution.py:15
  121.8 1.5 fusion.64
  124.3 2.5 %collective-permute-start.1 = (bf16[512,128]{1,0:T(8,128)(2,1)S(1)}, bf16[512,128]{1,0:T(8,128)(2,1)S(1)}, u32[]{:S(2)}, u32[]{:S(2)}) collective-permute-start(bf16[512,128]{1,0:T(8,128)(2,1)S(1)} %copy.37), channel_id=1, source_target_pairs={{0,1},{1,2},{2,3},{3,4},{4,5},{5,6},{6,7},{7,0},{8,9},{9,10},{10,1... | collective-permute-start | bytes 393224 | tf_op jit(solution)/shard_map/while/body/eval_jaxpr/ppermute | solution.py:15
  126.8 9.1 %collective-permute-done = bf16[512,128]{1,0:T(8,128)(2,1)S(1)} collective-permute-done((bf16[512,128]{1,0:T(8,128)(2,1)S(1)}, bf16[512,128]{1,0:T(8,128)(2,1)S(1)}, u32[]{:S(2)}, u32[]{:S(2)}) %collective-permute-start) | collective-permute-done | bytes 131104 | tf_op jit(solution)/shard_map/while/body/eval_jaxpr/ppermute | solution.py:15
  137.8 1.5 fusion.64
  140.3 3.2 %collective-permute-start.1 = (bf16[512,128]{1,0:T(8,128)(2,1)S(1)}, bf16[512,128]{1,0:T(8,128)(2,1)S(1)}, u32[]{:S(2)}, u32[]{:S(2)}) collective-permute-start(bf16[512,128]{1,0:T(8,128)(2,1)S(1)} %copy.37), channel_id=1, source_target_pairs={{0,1},{1,2},{2,3},{3,4},{4,5},{5,6},{6,7},{7,0},{8,9},{9,10},{10,1... | collective-permute-start | bytes 393224 | tf_op jit(solution)/shard_map/while/body/eval_jaxpr/ppermute | solution.py:15
  143.5 8.4 %collective-permute-done = bf16[512,128]{1,0:T(8,128)(2,1)S(1)} collective-permute-done((bf16[512,128]{1,0:T(8,128)(2,1)S(1)}, bf16[512,128]{1,0:T(8,128)(2,1)S(1)}, u32[]{:S(2)}, u32[]{:S(2)}) %collective-permute-start) | collective-permute-done | bytes 131104 | tf_op jit(solution)/shard_map/while/body/eval_jaxpr/ppermute | solution.py:15
  153.9 1.5 fusion.64
  157.8 10.2 %collective-permute-done = bf16[512,128]{1,0:T(8,128)(2,1)S(1)} collective-permute-done((bf16[512,128]{1,0:T(8,128)(2,1)S(1)}, bf16[512,128]{1,0:T(8,128)(2,1)S(1)}, u32[]{:S(2)}, u32[]{:S(2)}) %collective-permute-start) | collective-permute-done | bytes 131104 | tf_op jit(solution)/shard_map/while/body/eval_jaxpr/ppermute | solution.py:15
  172.4 1.5 collective-permute-start.1
  173.9 10.1 %collective-permute-done = bf16[512,128]{1,0:T(8,128)(2,1)S(1)} collective-permute-done((bf16[512,128]{1,0:T(8,128)(2,1)S(1)}, bf16[512,128]{1,0:T(8,128)(2,1)S(1)}, u32[]{:S(2)}, u32[]{:S(2)}) %collective-permute-start) | collective-permute-done | bytes 131104 | tf_op jit(solution)/shard_map/while/body/eval_jaxpr/ppermute | solution.py:15
  185.4 3.6 %conditional.3 = (f32[1024,128]{1,0:T(8,128)S(1)}, f32[512,128]{1,0:T(8,128)S(1)}, f32[512,128]{1,0:T(8,128)S(1)}) conditional(s32[]{:T(128)} %convert_element_type.66, f32[1024,128]{1,0:T(8,128)S(1)} %get-tuple-element.749, (bf16[1024,128]{1,0:T(8,128)(2,1)S(1)}, bf16[512,128]{1,0:T(8,128)(2,1)S(1)}, f32[1024]{0:T(1024)S(1)}, ...), branch_computations={%region_15.16_spmd, %region_16.17_spmd} | conditional | flops 675086336 | bytes 12984344 | solution.py:113
  185.4 1.7 exponential_select_fusion.1
  190.1 5.2 %collective-permute-done.4 = bf16[512,128]{1,0:T(8,128)(2,1)S(1)} collective-permute-done((bf16[512,128]{1,0:T(8,128)(2,1)S(1)}, bf16[512,128]{1,0:T(8,128)(2,1)S(1)}, u32[]{:S(2)}, u32[]{:S(2)}) %collective-permute-start.4) | collective-permute-done | bytes 131104 | tf_op jit(solution)/shard_map/ppermute | solution.py:15
  (264 shorter events, 50.8 us)
Async XLA Ops:
  7.2 27.8 %all-gather.2.cloned.1.call-start = ((), (), s32[]{:S(2)}) async-start(), calls=%async_computation | async-start | bytes 1179648 | tf_op jit(solution)/shard_map/all_gather | solution.py:67
  35.0 24.8 %copy-start.1 = (bf16[1,512,128]{2,1,0:T(8,128)(2,1)S(1)}, bf16[1,512,128]{2,1,0:T(8,128)(2,1)}, u32[]{:S(2)}) copy-start(bf16[1,512,128]{2,1,0:T(8,128)(2,1)} %param.19) | copy-start | bytes 393220
  65.1 24.1 %collective-permute-start.3 = (f32[512,128]{1,0:T(8,128)S(1)}, f32[512,128]{1,0:T(8,128)S(1)}, u32[]{:S(2)}, u32[]{:S(2)}) collective-permute-start(f32[512,128]{1,0:T(8,128)S(1)} %add.289), channel_id=1, source_target_pairs={{0,1},{1,2},{2,3},{3,4},{4,5},{5,6},{6,7},{7,0},{8,9},{9,10},{10,1... | collective-permute-start | bytes 786440 | tf_op jit(solution)/shard_map/while/body/eval_jaxpr/ppermute | solution.py:15
  65.4 23.8 %collective-permute-start.2 = (f32[512,128]{1,0:T(8,128)S(1)}, f32[512,128]{1,0:T(8,128)S(1)}, u32[]{:S(2)}, u32[]{:S(2)}) collective-permute-start(f32[512,128]{1,0:T(8,128)S(1)} %add.288), channel_id=1, source_target_pairs={{0,1},{1,2},{2,3},{3,4},{4,5},{5,6},{6,7},{7,0},{8,9},{9,10},{10,1... | collective-permute-start | bytes 786440 | tf_op jit(solution)/shard_map/while/body/eval_jaxpr/ppermute | solution.py:15
  69.3 18.5 %collective-permute-start = (bf16[512,128]{1,0:T(8,128)(2,1)S(1)}, bf16[512,128]{1,0:T(8,128)(2,1)S(1)}, u32[]{:S(2)}, u32[]{:S(2)}) collective-permute-start(bf16[512,128]{1,0:T(8,128)(2,1)S(1)} %copy.36), channel_id=1, source_target_pairs={{0,1},{1,2},{2,3},{3,4},{4,5},{5,6},{6,7},{7,0},{8,9},{9,10},{10,1... | collective-permute-start | bytes 393224 | tf_op jit(solution)/shard_map/while/body/eval_jaxpr/ppermute | solution.py:15
  73.7 15.5 %collective-permute-start.1 = (bf16[512,128]{1,0:T(8,128)(2,1)S(1)}, bf16[512,128]{1,0:T(8,128)(2,1)S(1)}, u32[]{:S(2)}, u32[]{:S(2)}) collective-permute-start(bf16[512,128]{1,0:T(8,128)(2,1)S(1)} %copy.37), channel_id=1, source_target_pairs={{0,1},{1,2},{2,3},{3,4},{4,5},{5,6},{6,7},{7,0},{8,9},{9,10},{10,1... | collective-permute-start | bytes 393224 | tf_op jit(solution)/shard_map/while/body/eval_jaxpr/ppermute | solution.py:15
  92.0 13.3 %collective-permute-start.3 = (f32[512,128]{1,0:T(8,128)S(1)}, f32[512,128]{1,0:T(8,128)S(1)}, u32[]{:S(2)}, u32[]{:S(2)}) collective-permute-start(f32[512,128]{1,0:T(8,128)S(1)} %add.289), channel_id=1, source_target_pairs={{0,1},{1,2},{2,3},{3,4},{4,5},{5,6},{6,7},{7,0},{8,9},{9,10},{10,1... | collective-permute-start | bytes 786440 | tf_op jit(solution)/shard_map/while/body/eval_jaxpr/ppermute | solution.py:15
  92.1 13.2 %collective-permute-start.2 = (f32[512,128]{1,0:T(8,128)S(1)}, f32[512,128]{1,0:T(8,128)S(1)}, u32[]{:S(2)}, u32[]{:S(2)}) collective-permute-start(f32[512,128]{1,0:T(8,128)S(1)} %add.288), channel_id=1, source_target_pairs={{0,1},{1,2},{2,3},{3,4},{4,5},{5,6},{6,7},{7,0},{8,9},{9,10},{10,1... | collective-permute-start | bytes 786440 | tf_op jit(solution)/shard_map/while/body/eval_jaxpr/ppermute | solution.py:15
  92.1 11.7 %collective-permute-start = (bf16[512,128]{1,0:T(8,128)(2,1)S(1)}, bf16[512,128]{1,0:T(8,128)(2,1)S(1)}, u32[]{:S(2)}, u32[]{:S(2)}) collective-permute-start(bf16[512,128]{1,0:T(8,128)(2,1)S(1)} %copy.36), channel_id=1, source_target_pairs={{0,1},{1,2},{2,3},{3,4},{4,5},{5,6},{6,7},{7,0},{8,9},{9,10},{10,1... | collective-permute-start | bytes 393224 | tf_op jit(solution)/shard_map/while/body/eval_jaxpr/ppermute | solution.py:15
  92.2 13.0 %collective-permute-start.1 = (bf16[512,128]{1,0:T(8,128)(2,1)S(1)}, bf16[512,128]{1,0:T(8,128)(2,1)S(1)}, u32[]{:S(2)}, u32[]{:S(2)}) collective-permute-start(bf16[512,128]{1,0:T(8,128)(2,1)S(1)} %copy.37), channel_id=1, source_target_pairs={{0,1},{1,2},{2,3},{3,4},{4,5},{5,6},{6,7},{7,0},{8,9},{9,10},{10,1... | collective-permute-start | bytes 393224 | tf_op jit(solution)/shard_map/while/body/eval_jaxpr/ppermute | solution.py:15
  108.0 13.3 %collective-permute-start.3 = (f32[512,128]{1,0:T(8,128)S(1)}, f32[512,128]{1,0:T(8,128)S(1)}, u32[]{:S(2)}, u32[]{:S(2)}) collective-permute-start(f32[512,128]{1,0:T(8,128)S(1)} %add.289), channel_id=1, source_target_pairs={{0,1},{1,2},{2,3},{3,4},{4,5},{5,6},{6,7},{7,0},{8,9},{9,10},{10,1... | collective-permute-start | bytes 786440 | tf_op jit(solution)/shard_map/while/body/eval_jaxpr/ppermute | solution.py:15
  108.1 13.2 %collective-permute-start.2 = (f32[512,128]{1,0:T(8,128)S(1)}, f32[512,128]{1,0:T(8,128)S(1)}, u32[]{:S(2)}, u32[]{:S(2)}) collective-permute-start(f32[512,128]{1,0:T(8,128)S(1)} %add.288), channel_id=1, source_target_pairs={{0,1},{1,2},{2,3},{3,4},{4,5},{5,6},{6,7},{7,0},{8,9},{9,10},{10,1... | collective-permute-start | bytes 786440 | tf_op jit(solution)/shard_map/while/body/eval_jaxpr/ppermute | solution.py:15
  108.2 11.7 %collective-permute-start = (bf16[512,128]{1,0:T(8,128)(2,1)S(1)}, bf16[512,128]{1,0:T(8,128)(2,1)S(1)}, u32[]{:S(2)}, u32[]{:S(2)}) collective-permute-start(bf16[512,128]{1,0:T(8,128)(2,1)S(1)} %copy.36), channel_id=1, source_target_pairs={{0,1},{1,2},{2,3},{3,4},{4,5},{5,6},{6,7},{7,0},{8,9},{9,10},{10,1... | collective-permute-start | bytes 393224 | tf_op jit(solution)/shard_map/while/body/eval_jaxpr/ppermute | solution.py:15
  108.3 13.0 %collective-permute-start.1 = (bf16[512,128]{1,0:T(8,128)(2,1)S(1)}, bf16[512,128]{1,0:T(8,128)(2,1)S(1)}, u32[]{:S(2)}, u32[]{:S(2)}) collective-permute-start(bf16[512,128]{1,0:T(8,128)(2,1)S(1)} %copy.37), channel_id=1, source_target_pairs={{0,1},{1,2},{2,3},{3,4},{4,5},{5,6},{6,7},{7,0},{8,9},{9,10},{10,1... | collective-permute-start | bytes 393224 | tf_op jit(solution)/shard_map/while/body/eval_jaxpr/ppermute | solution.py:15
  124.1 13.3 %collective-permute-start.3 = (f32[512,128]{1,0:T(8,128)S(1)}, f32[512,128]{1,0:T(8,128)S(1)}, u32[]{:S(2)}, u32[]{:S(2)}) collective-permute-start(f32[512,128]{1,0:T(8,128)S(1)} %add.289), channel_id=1, source_target_pairs={{0,1},{1,2},{2,3},{3,4},{4,5},{5,6},{6,7},{7,0},{8,9},{9,10},{10,1... | collective-permute-start | bytes 786440 | tf_op jit(solution)/shard_map/while/body/eval_jaxpr/ppermute | solution.py:15
  124.2 13.2 %collective-permute-start.2 = (f32[512,128]{1,0:T(8,128)S(1)}, f32[512,128]{1,0:T(8,128)S(1)}, u32[]{:S(2)}, u32[]{:S(2)}) collective-permute-start(f32[512,128]{1,0:T(8,128)S(1)} %add.288), channel_id=1, source_target_pairs={{0,1},{1,2},{2,3},{3,4},{4,5},{5,6},{6,7},{7,0},{8,9},{9,10},{10,1... | collective-permute-start | bytes 786440 | tf_op jit(solution)/shard_map/while/body/eval_jaxpr/ppermute | solution.py:15
  124.2 11.7 %collective-permute-start = (bf16[512,128]{1,0:T(8,128)(2,1)S(1)}, bf16[512,128]{1,0:T(8,128)(2,1)S(1)}, u32[]{:S(2)}, u32[]{:S(2)}) collective-permute-start(bf16[512,128]{1,0:T(8,128)(2,1)S(1)} %copy.36), channel_id=1, source_target_pairs={{0,1},{1,2},{2,3},{3,4},{4,5},{5,6},{6,7},{7,0},{8,9},{9,10},{10,1... | collective-permute-start | bytes 393224 | tf_op jit(solution)/shard_map/while/body/eval_jaxpr/ppermute | solution.py:15
  124.3 13.0 %collective-permute-start.1 = (bf16[512,128]{1,0:T(8,128)(2,1)S(1)}, bf16[512,128]{1,0:T(8,128)(2,1)S(1)}, u32[]{:S(2)}, u32[]{:S(2)}) collective-permute-start(bf16[512,128]{1,0:T(8,128)(2,1)S(1)} %copy.37), channel_id=1, source_target_pairs={{0,1},{1,2},{2,3},{3,4},{4,5},{5,6},{6,7},{7,0},{8,9},{9,10},{10,1... | collective-permute-start | bytes 393224 | tf_op jit(solution)/shard_map/while/body/eval_jaxpr/ppermute | solution.py:15
  140.1 13.3 %collective-permute-start.3 = (f32[512,128]{1,0:T(8,128)S(1)}, f32[512,128]{1,0:T(8,128)S(1)}, u32[]{:S(2)}, u32[]{:S(2)}) collective-permute-start(f32[512,128]{1,0:T(8,128)S(1)} %add.289), channel_id=1, source_target_pairs={{0,1},{1,2},{2,3},{3,4},{4,5},{5,6},{6,7},{7,0},{8,9},{9,10},{10,1... | collective-permute-start | bytes 786440 | tf_op jit(solution)/shard_map/while/body/eval_jaxpr/ppermute | solution.py:15
  140.2 13.2 %collective-permute-start.2 = (f32[512,128]{1,0:T(8,128)S(1)}, f32[512,128]{1,0:T(8,128)S(1)}, u32[]{:S(2)}, u32[]{:S(2)}) collective-permute-start(f32[512,128]{1,0:T(8,128)S(1)} %add.288), channel_id=1, source_target_pairs={{0,1},{1,2},{2,3},{3,4},{4,5},{5,6},{6,7},{7,0},{8,9},{9,10},{10,1... | collective-permute-start | bytes 786440 | tf_op jit(solution)/shard_map/while/body/eval_jaxpr/ppermute | solution.py:15
  140.3 11.7 %collective-permute-start = (bf16[512,128]{1,0:T(8,128)(2,1)S(1)}, bf16[512,128]{1,0:T(8,128)(2,1)S(1)}, u32[]{:S(2)}, u32[]{:S(2)}) collective-permute-start(bf16[512,128]{1,0:T(8,128)(2,1)S(1)} %copy.36), channel_id=1, source_target_pairs={{0,1},{1,2},{2,3},{3,4},{4,5},{5,6},{6,7},{7,0},{8,9},{9,10},{10,1... | collective-permute-start | bytes 393224 | tf_op jit(solution)/shard_map/while/body/eval_jaxpr/ppermute | solution.py:15
  140.3 13.0 %collective-permute-start.1 = (bf16[512,128]{1,0:T(8,128)(2,1)S(1)}, bf16[512,128]{1,0:T(8,128)(2,1)S(1)}, u32[]{:S(2)}, u32[]{:S(2)}) collective-permute-start(bf16[512,128]{1,0:T(8,128)(2,1)S(1)} %copy.37), channel_id=1, source_target_pairs={{0,1},{1,2},{2,3},{3,4},{4,5},{5,6},{6,7},{7,0},{8,9},{9,10},{10,1... | collective-permute-start | bytes 393224 | tf_op jit(solution)/shard_map/while/body/eval_jaxpr/ppermute | solution.py:15
  156.1 13.3 %collective-permute-start.3 = (f32[512,128]{1,0:T(8,128)S(1)}, f32[512,128]{1,0:T(8,128)S(1)}, u32[]{:S(2)}, u32[]{:S(2)}) collective-permute-start(f32[512,128]{1,0:T(8,128)S(1)} %add.289), channel_id=1, source_target_pairs={{0,1},{1,2},{2,3},{3,4},{4,5},{5,6},{6,7},{7,0},{8,9},{9,10},{10,1... | collective-permute-start | bytes 786440 | tf_op jit(solution)/shard_map/while/body/eval_jaxpr/ppermute | solution.py:15
  156.2 13.2 %collective-permute-start.2 = (f32[512,128]{1,0:T(8,128)S(1)}, f32[512,128]{1,0:T(8,128)S(1)}, u32[]{:S(2)}, u32[]{:S(2)}) collective-permute-start(f32[512,128]{1,0:T(8,128)S(1)} %add.288), channel_id=1, source_target_pairs={{0,1},{1,2},{2,3},{3,4},{4,5},{5,6},{6,7},{7,0},{8,9},{9,10},{10,1... | collective-permute-start | bytes 786440 | tf_op jit(solution)/shard_map/while/body/eval_jaxpr/ppermute | solution.py:15
  156.3 11.7 %collective-permute-start = (bf16[512,128]{1,0:T(8,128)(2,1)S(1)}, bf16[512,128]{1,0:T(8,128)(2,1)S(1)}, u32[]{:S(2)}, u32[]{:S(2)}) collective-permute-start(bf16[512,128]{1,0:T(8,128)(2,1)S(1)} %copy.36), channel_id=1, source_target_pairs={{0,1},{1,2},{2,3},{3,4},{4,5},{5,6},{6,7},{7,0},{8,9},{9,10},{10,1... | collective-permute-start | bytes 393224 | tf_op jit(solution)/shard_map/while/body/eval_jaxpr/ppermute | solution.py:15
  156.4 13.0 %collective-permute-start.1 = (bf16[512,128]{1,0:T(8,128)(2,1)S(1)}, bf16[512,128]{1,0:T(8,128)(2,1)S(1)}, u32[]{:S(2)}, u32[]{:S(2)}) collective-permute-start(bf16[512,128]{1,0:T(8,128)(2,1)S(1)} %copy.37), channel_id=1, source_target_pairs={{0,1},{1,2},{2,3},{3,4},{4,5},{5,6},{6,7},{7,0},{8,9},{9,10},{10,1... | collective-permute-start | bytes 393224 | tf_op jit(solution)/shard_map/while/body/eval_jaxpr/ppermute | solution.py:15
  172.2 13.3 %collective-permute-start.3 = (f32[512,128]{1,0:T(8,128)S(1)}, f32[512,128]{1,0:T(8,128)S(1)}, u32[]{:S(2)}, u32[]{:S(2)}) collective-permute-start(f32[512,128]{1,0:T(8,128)S(1)} %add.289), channel_id=1, source_target_pairs={{0,1},{1,2},{2,3},{3,4},{4,5},{5,6},{6,7},{7,0},{8,9},{9,10},{10,1... | collective-permute-start | bytes 786440 | tf_op jit(solution)/shard_map/while/body/eval_jaxpr/ppermute | solution.py:15
  172.3 13.2 %collective-permute-start.2 = (f32[512,128]{1,0:T(8,128)S(1)}, f32[512,128]{1,0:T(8,128)S(1)}, u32[]{:S(2)}, u32[]{:S(2)}) collective-permute-start(f32[512,128]{1,0:T(8,128)S(1)} %add.288), channel_id=1, source_target_pairs={{0,1},{1,2},{2,3},{3,4},{4,5},{5,6},{6,7},{7,0},{8,9},{9,10},{10,1... | collective-permute-start | bytes 786440 | tf_op jit(solution)/shard_map/while/body/eval_jaxpr/ppermute | solution.py:15
  172.3 11.7 %collective-permute-start = (bf16[512,128]{1,0:T(8,128)(2,1)S(1)}, bf16[512,128]{1,0:T(8,128)(2,1)S(1)}, u32[]{:S(2)}, u32[]{:S(2)}) collective-permute-start(bf16[512,128]{1,0:T(8,128)(2,1)S(1)} %copy.36), channel_id=1, source_target_pairs={{0,1},{1,2},{2,3},{3,4},{4,5},{5,6},{6,7},{7,0},{8,9},{9,10},{10,1... | collective-permute-start | bytes 393224 | tf_op jit(solution)/shard_map/while/body/eval_jaxpr/ppermute | solution.py:15
  172.4 13.0 %collective-permute-start.1 = (bf16[512,128]{1,0:T(8,128)(2,1)S(1)}, bf16[512,128]{1,0:T(8,128)(2,1)S(1)}, u32[]{:S(2)}, u32[]{:S(2)}) collective-permute-start(bf16[512,128]{1,0:T(8,128)(2,1)S(1)} %copy.37), channel_id=1, source_target_pairs={{0,1},{1,2},{2,3},{3,4},{4,5},{5,6},{6,7},{7,0},{8,9},{9,10},{10,1... | collective-permute-start | bytes 393224 | tf_op jit(solution)/shard_map/while/body/eval_jaxpr/ppermute | solution.py:15
  189.1 6.2 %collective-permute-start.4 = (bf16[512,128]{1,0:T(8,128)(2,1)S(1)}, bf16[512,128]{1,0:T(8,128)(2,1)S(1)}, u32[]{:S(2)}, u32[]{:S(2)}) collective-permute-start(bf16[512,128]{1,0:T(8,128)(2,1)S(1)} %add_convert_fusion.1), channel_id=1, source_target_pairs={{0,1},{1,2},{2,3},{3,4},{4,5},{5,6},{6,7},{7,0},{8,9},{9,10},{10,1... | collective-permute-start | bytes 393224 | tf_op jit(solution)/shard_map/ppermute | solution.py:15
  189.2 7.5 %collective-permute-start.5 = (bf16[512,128]{1,0:T(8,128)(2,1)S(1)}, bf16[512,128]{1,0:T(8,128)(2,1)S(1)}, u32[]{:S(2)}, u32[]{:S(2)}) collective-permute-start(bf16[512,128]{1,0:T(8,128)(2,1)S(1)} %add_convert_fusion), channel_id=1, source_target_pairs={{0,1},{1,2},{2,3},{3,4},{4,5},{5,6},{6,7},{7,0},{8,9},{9,10},{10,1... | collective-permute-start | bytes 393224 | tf_op jit(solution)/shard_map/ppermute | solution.py:15
  (2 other events, 47.9 us)
Sparse Core Ops, SparseCore 0:
  10.2 24.7 all-gather.1
where the time goes:
time: 205 us
  waiting for transfers between devices  90.3 us (44%)
  other arithmetic  26.6 us (13%)
  starting transfers between devices  24.2 us (12%)
  between operations  14.8 us (7%)
  blocking collectives  14.5 us (7%)
  local copies, waits for them, and re-layouts  14 us (7%)
  loops' own time  11.5 us (6%)
  matrix products  8.9 us (4%)
    ppermute x30, waiting for transfers between devices, from_behind(): return lax.ppermute(value, axis, pairs)  85.8 us
    ppermute x30, starting transfers between devices, from_behind(): return lax.ppermute(value, axis, pairs)  24.2 us
    all_gather x1, blocking collectives, per_device(): seg_whole = lax.all_gather(segment_ids, 'ctx', axis=1, tiled=True)[0]  14.5 us
    reduce_or x8, other arithmetic, grads_tile(): return lax.cond(jnp.any(visible), grads_compute_tile, grads_skip_tile)  12.7 us
    reduce_or x8, other arithmetic, stats_one_block(): return lax.cond(jnp.any(visible), stats_compute_tile, stats_skip_tile)  11 us
    dot_general x6, matrix products, contract_cols(): lax.dot_general(left, right, (((1,), (1,)), ((), ())), preferred_element_...  6.07 us
    another operation x1, loops' own time, per_device(): lax.fori_loop(0, number, stats_one_block, (top_start, total_start))  5.84 us
    another operation x1, loops' own time, per_device(): lax.fori_loop(0, rank_count - 1, pass_step, (keys[0], values[0], zeros_sh...  5.24 us
  transfers between devices with their start and end apart: 31, of which 17 were waited for; matrix products, arithmetic and copies ran while one was open for 4% of the time, Pallas kernels for 0%

commit v1 on v0

v1 whole, which is shorter than its diff:
```python
import functools
import math

import jax
import jax.numpy as jnp
from jax import lax
from jax.experimental import pallas as pl
from jax.experimental.pallas import tpu as pltpu
from jax.sharding import PartitionSpec as P

HD = 128
SEG_MOST = 1024
CORES = 2
LOW = -1e30
FLOOR = -1e29
KEEP_BYTES = 20 * 1024 * 1024
F32 = jnp.float32
BF16 = jnp.bfloat16


def push(src, dst, send, recv, rank):
    return pltpu.make_async_remote_copy(
        src_ref=src,
        dst_ref=dst,
        send_sem=send,
        recv_sem=recv,
        device_id={"ctx": rank},
        device_id_type=pl.DeviceIdType.MESH,
    )


def fused(
    ranks, look, chunk, keep,
    q_ref, k_ref, v_ref, do_ref, o_ref, seg_ref, flag_ref,
    dq_ref, dk_ref, dv_ref,
    kbuf, vbuf, ebuf, tops, qcols, qrows, docols, dorows, reach, odot, top, total, lse, dqt,
    gpart, sib_out, sib_in, ch_out, ch_in, low_in, segs,
    k_up, k_side, k_down, k_recv, v_up, v_side, v_down, v_recv,
    gs_send, gs_recv, gc_send, gc_recv, gl_send, gl_recv, seg_send, seg_recv,
):
    chips = ranks // CORES
    key_rows = k_ref.shape[0]
    query_rows = q_ref.shape[0]
    heads = q_ref.shape[1] // HD
    cols = query_rows * heads
    parts = key_rows // chunk
    scale = 1.0 / math.sqrt(HD)
    factor = scale * math.log2(math.e)
    me = lax.axis_index("ctx")
    chip = me // CORES
    core = me % CORES
    side = chip * CORES + (1 - core)
    is_top = chip == chips - 1
    not_top = chip < chips - 1
    has_low = chip > 0
    own_slot = me
    reach_ranks = max(look, CORES)

    barrier = pltpu.get_barrier_semaphore()
    there = jnp.int32(0)
    for d in range(1, reach_ranks + 1):
        @pl.when(me + d < ranks)
        def _():
            pl.semaphore_signal(barrier, inc=1, device_id={"ctx": me + d},
                                device_id_type=pl.DeviceIdType.MESH)

        @pl.when(me - d >= 0)
        def _():
            pl.semaphore_signal(barrier, inc=1, device_id={"ctx": me - d},
                                device_id_type=pl.DeviceIdType.MESH)

        there = there + jnp.where(me + d < ranks, 1, 0) + jnp.where(me - d >= 0, 1, 0)
    kbuf[own_slot] = k_ref[...]
    vbuf[own_slot] = v_ref[...]
    pl.semaphore_wait(barrier, there)

    def up(buf, sems, recv, w):
        slot = w * CORES + core
        return push(buf.at[slot], buf.at[slot], sems.at[w], recv.at[slot], me + CORES)

    def across(buf, sems, recv, w):
        slot = w * CORES + core
        return push(buf.at[slot], buf.at[slot], sems.at[w], recv.at[slot], side)

    def down(buf, sems, recv):
        return push(buf.at[own_slot], buf.at[own_slot], sems.at[0], recv.at[own_slot], me - CORES)

    def arrived(buf, sems, recv, slot):
        push(buf.at[slot], buf.at[slot], sems.at[0], recv.at[slot], side).wait_recv()

    def seg_copy(d, rank):
        return push(seg_ref, segs.at[d - 1], seg_send.at[d - 1], seg_recv.at[d - 1], rank)

    def grad_side(kind, w):
        return push(sib_out.at[kind, w], sib_in.at[kind, w], gs_send.at[kind, w], gs_recv.at[kind, w], side)

    def grad_down(kind, w):
        return push(ch_out.at[kind, w], ch_in.at[kind, w], gc_send.at[kind, w], gc_recv.at[kind, w], me - CORES)

    def grad_up(kind):
        return push(ch_out.at[kind, chip + 1], low_in.at[kind], gl_send.at[kind], gl_recv.at[kind], me + CORES)

    @pl.when(not_top)
    def _():
        up(kbuf, k_up, k_recv, chip).start()

    across(kbuf, k_side, k_recv, chip).start()
    for d in range(1, look + 1):
        @pl.when(me - d >= 0)
        def _():
            seg_copy(d, me - d).start()

    @pl.when(has_low)
    def _():
        down(kbuf, k_down, k_recv).start()
        down(vbuf, v_down, v_recv).start()

    across(vbuf, v_side, v_recv, chip).start()

    for h in range(heads):
        at = slice(h * HD, (h + 1) * HD)
        rows = slice(h * query_rows, (h + 1) * query_rows)
        q_h = q_ref[:, at]
        do_h = do_ref[:, at]
        qrows[rows, :] = q_h
        dorows[rows, :] = do_h
        qcols[:, rows] = q_h.T
        docols[:, rows] = do_h.T
        odot[:, rows] = jnp.sum((do_h.astype(F32) * o_ref[:, at].astype(F32)).T, axis=0, keepdims=True)
    top[...] = jnp.full(top.shape, FLOOR, F32)
    total[...] = jnp.zeros(total.shape, F32)
    dqt[...] = jnp.zeros(dqt.shape, F32)

    for d in range(1, look + 1):
        @pl.when(me + d < ranks)
        def _():
            seg_copy(d, side).wait_recv()

        @pl.when(me + d >= ranks)
        def _():
            segs[d - 1] = jnp.full(seg_ref.shape, 1 << 20, jnp.int32)

    seg_q = seg_ref[:, key_rows - query_rows:].astype(F32)
    seg_col = jnp.broadcast_to(seg_q, (HD, query_rows)).T
    counts = jnp.zeros((query_rows, HD), F32)
    for d in range(look + 1):
        for j in range(key_rows // HD):
            at = slice(j * HD, (j + 1) * HD)
            piece = (seg_ref[:, at] if d == 0 else segs[d - 1, :, at]).astype(F32)
            counts = counts + jnp.where(piece <= seg_col, 1.0, 0.0)
    count = jnp.sum(counts, axis=1, keepdims=True)
    segments = flag_ref.shape[1]
    ids = lax.broadcasted_iota(jnp.int32, (query_rows, segments), 1).astype(F32)
    flags = jnp.broadcast_to(flag_ref[...].astype(F32), (query_rows, segments))
    framed = jnp.sum(jnp.where(ids == seg_col[:, :1], flags, 0.0), axis=1, keepdims=True)
    local = (key_rows - query_rows) + lax.broadcasted_iota(jnp.int32, (query_rows, 1), 0).astype(F32)
    last = jnp.where(framed == 1.0, count - 1.0, local)
    last_row = jnp.broadcast_to(last, (query_rows, HD)).T[:1, :].astype(jnp.int32) + me * key_rows
    for h in range(heads):
        reach[:, h * query_rows:(h + 1) * query_rows] = last_row

    def rows_of(part):
        return pl.ds(pl.multiple_of(part * chunk, chunk), chunk)

    def scores_of(slot, part, masked):
        s = jnp.dot(kbuf[slot, rows_of(part), :], qcols[...], preferred_element_type=F32) * factor
        if masked:
            first = slot * key_rows + part * chunk
            pos = first + lax.broadcasted_iota(jnp.int32, (chunk, cols), 0)
            s = jnp.where(pos <= reach[...], s, LOW)
        return s

    def stats(slot, masked):
        @pl.loop(0, parts)
        def _(part):
            s = scores_of(slot, part, masked)
            here = jnp.maximum(jnp.max(s, axis=0, keepdims=True), FLOOR)
            e = jnp.exp2(s - here)
            if keep:
                ebuf[slot, rows_of(part), :] = e
                tops[slot * parts + part] = here
            old = top[...]
            new = jnp.maximum(old, here)
            total[...] = total[...] * jnp.exp2(old - new) + (
                jnp.sum(e, axis=0, keepdims=True) * jnp.exp2(here - new))
            top[...] = new

    def chip_stats(w, masked):
        @pl.loop(0, CORES)
        def _(b):
            slot = w * CORES + (core + b) % CORES

            @pl.when(b == 1)
            def _():
                arrived(kbuf, k_side, k_recv, slot)

            stats(slot, masked)

    def probs_of(slot, part, masked):
        if keep:
            return ebuf[slot, rows_of(part), :] * jnp.exp2(tops[slot * parts + part] - lse[...])
        return jnp.exp2(scores_of(slot, part, masked) - lse[...])

    def send_side(kind, w):
        sib_out[kind, w] = gpart[kind, w * CORES + (1 - core)].astype(BF16)
        grad_side(kind, w).start()

    def value_grads(w, masked):
        @pl.loop(0, CORES * parts)
        def _(i):
            slot = w * CORES + i // parts
            part = i % parts
            p = probs_of(slot, part, masked).astype(BF16)
            gpart[0, slot, rows_of(part), :] = jnp.dot(p, dorows[...], preferred_element_type=F32)

        send_side(0, w)

    def key_grads(w, masked):
        @pl.loop(0, CORES)
        def _(b):
            slot = w * CORES + (core + b) % CORES

            @pl.when(b == 1)
            def _():
                arrived(vbuf, v_side, v_recv, slot)

            @pl.loop(0, parts)
            def _(part):
                p = probs_of(slot, part, masked)
                dp = jnp.dot(vbuf[slot, rows_of(part), :], docols[...], preferred_element_type=F32)
                ds = (p * (dp - odot[...])).astype(BF16)
                gpart[1, slot, rows_of(part), :] = scale * jnp.dot(ds, qrows[...], preferred_element_type=F32)
                dqt[...] += jnp.dot(kbuf[slot, rows_of(part), :].T, ds, preferred_element_type=F32)

        send_side(1, w)

    def summed(kind, w):
        grad_side(kind, w).wait_recv()
        return gpart[kind, w * CORES + core] + sib_in[kind, w].astype(F32)

    def hand_down(kind, w):
        ch_out[kind, w] = summed(kind, w).astype(BF16)

        @pl.when(not_top)
        def _():
            grad_down(kind, w).wait_recv()
            ch_out[kind, w] = (summed_again(kind, w) + ch_in[kind, w].astype(F32)).astype(BF16)

        grad_down(kind, w).start()

    def summed_again(kind, w):
        return gpart[kind, w * CORES + core] + sib_in[kind, w].astype(F32)

    @pl.when(jnp.logical_and(not_top, chip == 0))
    def _():
        up(vbuf, v_up, v_recv, chip).start()

    chip_stats(chip, True)

    @pl.loop(1, chip + 1)
    def _(s):
        w = chip - s
        arrived(kbuf, k_side, k_recv, w * CORES + core)

        @pl.when(not_top)
        def _():
            up(kbuf, k_up, k_recv, w).start()

        across(kbuf, k_side, k_recv, w).start()

        @pl.when(jnp.logical_and(not_top, w == 0))
        def _():
            up(vbuf, v_up, v_recv, chip).start()

        chip_stats(w, False)

    @pl.when(not_top)
    def _():
        arrived(kbuf, k_side, k_recv, (chip + 1) * CORES + core)
        across(kbuf, k_side, k_recv, chip + 1).start()
        chip_stats(chip + 1, True)

    lse[...] = top[...] + jnp.log(total[...]) * math.log2(math.e)

    @pl.loop(0, chip)
    def _(t):
        w = chip - 1 - t
        value_grads(w, False)

        @pl.when(not_top)
        def _():
            arrived(vbuf, v_side, v_recv, w * CORES + core)
            up(vbuf, v_up, v_recv, w).start()
            across(vbuf, v_side, v_recv, w).start()

        @pl.when(jnp.logical_and(is_top, t > 0))
        def _():
            hand_down(0, w + 1)

    @pl.when(jnp.logical_and(is_top, has_low))
    def _():
        hand_down(0, 0)

    @pl.loop(0, chip)
    def _(t):
        w = chip - 1 - t

        @pl.when(is_top)
        def _():
            arrived(vbuf, v_side, v_recv, w * CORES + core)
            across(vbuf, v_side, v_recv, w).start()

        key_grads(w, False)

        @pl.when(jnp.logical_and(is_top, t > 0))
        def _():
            hand_down(1, w + 1)

        @pl.when(not_top)
        def _():
            hand_down(0, w)

    @pl.when(jnp.logical_and(is_top, has_low))
    def _():
        hand_down(1, 0)

    end = jnp.where(not_top, 2, 1)

    @pl.loop(0, end)
    def _(t):
        w = chip + end - 1 - t
        value_grads(w, True)

        @pl.when(w > chip)
        def _():
            arrived(vbuf, v_side, v_recv, w * CORES + core)
            across(vbuf, v_side, v_recv, w).start()

        key_grads(w, True)

        @pl.when(w > chip)
        def _():
            for kind in range(2):
                ch_out[kind, w] = summed(kind, w).astype(BF16)
                grad_up(kind).start()

    @pl.when(not_top)
    def _():
        @pl.loop(0, chip)
        def _(t):
            hand_down(1, chip - 1 - t)

    for h in range(heads):
        rows = slice(h * query_rows, (h + 1) * query_rows)
        dq_ref[:, h * HD:(h + 1) * HD] = (dqt[:, rows].T * scale).astype(BF16)

    for kind, out in ((0, dv_ref), (1, dk_ref)):
        gpart[kind, own_slot] = summed(kind, chip)

        @pl.when(has_low)
        def _():
            push(low_in.at[kind], low_in.at[kind], gl_send.at[kind], gl_recv.at[kind], side).wait_recv()
            gpart[kind, own_slot] = gpart[kind, own_slot] + low_in[kind].astype(F32)

        @pl.when(not_top)
        def _():
            grad_down(kind, chip).wait_recv()
            gpart[kind, own_slot] = gpart[kind, own_slot] + ch_in[kind, chip].astype(F32)

        out[...] = gpart[kind, own_slot].astype(BF16)

    for d in range(1, look + 1):
        @pl.when(me - d >= 0)
        def _():
            seg_copy(d, side).wait_send()

    @pl.when(has_low)
    def _():
        down(kbuf, k_down, k_recv).wait_send()
        down(vbuf, v_down, v_recv).wait_send()

    @pl.when(not_top)
    def _():
        for kind in range(2):
            grad_up(kind).wait_send()

    @pl.loop(0, chip + end)
    def _(w):
        across(kbuf, k_side, k_recv, w).wait_send()
        across(vbuf, v_side, v_recv, w).wait_send()
        for kind in range(2):
            grad_side(kind, w).wait_send()

        @pl.when(jnp.logical_and(not_top, w <= chip))
        def _():
            up(kbuf, k_up, k_recv, w).wait_send()
            up(vbuf, v_up, v_recv, w).wait_send()

        @pl.when(w < chip)
        def _():
            for kind in range(2):
                grad_down(kind, w).wait_send()


def per_device(queries, keys, values, grad_out, saved_out, segment_ids, frame_flags):
    ranks = lax.axis_size("ctx")
    chips = ranks // CORES
    key_rows = keys.shape[1]
    query_rows, width = queries.shape[1:]
    cols = query_rows * (width // HD)
    look = (SEG_MOST + key_rows - 2) // key_rows
    assert look <= CORES and ranks % CORES == 0
    chunk = math.gcd(key_rows, 256)
    parts = key_rows // chunk
    keep = ranks * key_rows * cols * 4 <= KEEP_BYTES
    kept = ranks if keep else 1
    dma = pltpu.SemaphoreType.DMA
    block = (key_rows, HD)
    grads = (2, chips) + block
    vmem = pl.BlockSpec(memory_space=pltpu.VMEM)
    grad_queries, grad_keys, grad_values = pl.pallas_call(
        functools.partial(fused, ranks, look, chunk, keep),
        out_shape=(
            jax.ShapeDtypeStruct((query_rows, width), BF16),
            jax.ShapeDtypeStruct(block, BF16),
            jax.ShapeDtypeStruct(block, BF16),
        ),
        in_specs=[vmem] * 7,
        out_specs=(vmem,) * 3,
        scratch_shapes=[
            pltpu.VMEM((ranks,) + block, BF16),
            pltpu.VMEM((ranks,) + block, BF16),
            pltpu.VMEM((kept, key_rows, cols), F32) if keep else pltpu.VMEM((8, 128), F32),
            pltpu.VMEM((kept * parts, 1, cols), F32),
            pltpu.VMEM((HD, cols), BF16),
            pltpu.VMEM((cols, HD), BF16),
            pltpu.VMEM((HD, cols), BF16),
            pltpu.VMEM((cols, HD), BF16),
            pltpu.VMEM((1, cols), jnp.int32),
            pltpu.VMEM((1, cols), F32),
            pltpu.VMEM((1, cols), F32),
            pltpu.VMEM((1, cols), F32),
            pltpu.VMEM((1, cols), F32),
            pltpu.VMEM((HD, cols), F32),
            pltpu.VMEM((2, ranks) + block, F32),
            pltpu.VMEM(grads, BF16),
            pltpu.VMEM(grads, BF16),
            pltpu.VMEM(grads, BF16),
            pltpu.VMEM(grads, BF16),
            pltpu.VMEM((2,) + block, BF16),
            pltpu.VMEM((look, 1, key_rows), jnp.int32),
            dma((chips,)), dma((chips,)), dma((1,)), dma((ranks,)),
            dma((chips,)), dma((chips,)), dma((1,)), dma((ranks,)),
            dma((2, chips)), dma((2, chips)), dma((2, chips)), dma((2, chips)),
            dma((2,)), dma((2,)), dma((look,)), dma((look,)),
        ],
        compiler_params=pltpu.CompilerParams(
            collective_id=0, has_side_effects=True, vmem_limit_bytes=60 * 1024 * 1024
        ),
        cost_estimate=pl.CostEstimate(
            flops=12 * cols * ranks * key_rows * HD,
            bytes_accessed=8 * cols * HD,
            transcendentals=cols * ranks * key_rows,
        ),
    )(queries[0], keys[0], values[0], grad_out[0], saved_out[0], segment_ids, frame_flags)
    return grad_queries[None], grad_keys[None], grad_values[None]


def solution(mesh):
    return jax.shard_map(
        per_device,
        mesh=mesh,
        in_specs=(
            P("dp", "ctx", None),
            P("dp", "ctx", None),
            P("dp", "ctx", None),
            P("dp", "ctx", None),
            P("dp", "ctx", None),
            P("dp", "ctx"),
            P("dp", None),
        ),
        out_specs=(P("dp", "ctx", None), P("dp", "ctx", None), P("dp", "ctx", None)),
        check_vma=False,
    )
```

time: 205 us -> 61.4 us (0.30)
  waiting for transfers between devices: 90.3 us -> 0 us
  Pallas kernels: 0 us -> 57.3 us
  other arithmetic: 26.6 us -> 0 us
  starting transfers between devices: 24.2 us -> 0 us
  blocking collectives: 14.5 us -> 0 us
  between operations: 14.8 us -> 0.65 us
  loops' own time: 11.5 us -> 0 us
  local copies, waits for them, and re-layouts: 14 us -> 3.31 us
  matrix products: 8.9 us -> 0 us
    ppermute x30 -> x0, waiting for transfers between devices: 85.8 us -> none  [from_behind(): return lax.ppermute(value, axis, pairs)]
    pallas_call x0 -> x1, Pallas kernels: none -> 57.3 us  [per_device(): pl.pallas_call(functools.partial(fused, ranks, look, chunk, keep), out_sh...]
    ppermute x30 -> x0, starting transfers between devices: 24.2 us -> none  [from_behind(): return lax.ppermute(value, axis, pairs)]
    reduce_or x16 -> x0, other arithmetic: 23.7 us -> none  [the longest x8 12.7 us: grads_tile(): return lax.cond(jnp.any(visible), grads_compute_tile, grads_skip_tile)]
    all_gather x1 -> x0, blocking collectives: 14.5 us -> none  [per_device(): seg_whole = lax.all_gather(segment_ids, 'ctx', axis=1, tiled=True)[0]]
    another operation x18 -> x0, loops' own time: 11.5 us -> none  [the longest x1 5.84 us: per_device(): lax.fori_loop(0, number, stats_one_block, (top_start, total_start))]
    dot_general x12 -> x0, matrix products: 8.9 us -> none  [the longest x6 6.07 us: contract_cols(): lax.dot_general(left, right, (((1,), (1,)), ((), ())), preferred_element_...]
    all_gather x1 -> x0, waiting for transfers between devices: 4.41 us -> none  [per_device(): key_piece = lax.all_gather(keys, 'ctx', axis=1, tiled=True)]
  transfers between devices with their start and end apart: 31 -> 0, of which waited for: 17 -> 0; matrix products, arithmetic and copies ran while one was open for 4% -> 0% of each run, Pallas kernels for 0% -> 0%
where the time goes in v1:
time: 61.4 us; the launch traced here: 61.3 us
  Pallas kernels  57.3 us (93%)
  local copies, waits for them, and re-layouts  3.31 us (5%)
  between operations  0.65 us (1%)
    pallas_call x1, Pallas kernels, per_device(): pl.pallas_call(functools.partial(fused, ranks, look, chunk, keep), out_sh...  57.3 us
    unnamed x7, local copies, waits for them, and re-layouts  3.31 us

profile of v1, /device:TPU:0, one launch (start us, length us, event | category | flops | bytes accessed | tf_op | source)
XLA Modules:
  0.0 61.3 jit_solution(3359765792783981292)
XLA Ops:
  0.6 57.3 %shard_map.94 = (bf16[128,1024]{1,0:T(8,128)(2,1)}, bf16[512,128]{1,0:T(8,128)(2,1)}, bf16[512,128]{1,0:T(8,128)(2,1)}) custom-call(bf16[128,1024]{1,0:T(8,128)(2,1)} %bitcast.11, bf16[512,128]{1,0:T(8,128)(2,1)} %bitcast.14, bf16[512,128]{1,0:T(8,128)(2,1)} %bitcast.15, bf16[128,1024]{1,0:T(8,128)(2,1)} %bitcast.12, bf16[128,1024]{1,0:T(8,128)(2,1)} %bitcast.13, ...), custom_call_target="tpu_custom_call" | custom-call | flops 6442450944 | bytes 1048576 | tf_op jit(solution)/shard_map/pallas_call | solution.py:421
  57.9 0.0 copy-start.1
  57.9 1.7 %copy.13 = bf16[1,128,1024]{2,1,0:T(8,128)(2,1)} copy(bf16[1,128,1024]{2,1,0:T(8,128)(2,1)} %bitcast.8) | data formatting | bytes 524288
  59.7 0.0 copy-done.1
  59.7 0.0 copy-start
  59.7 0.7 %copy.14 = bf16[1,512,128]{2,1,0:T(8,128)(2,1)} copy(bf16[1,512,128]{2,1,0:T(8,128)(2,1)S(1)} %bitcast.10) | data formatting | bytes 262144
  60.3 0.3 copy-done
  60.6 0.7 %copy.15 = bf16[1,512,128]{2,1,0:T(8,128)(2,1)} copy(bf16[1,512,128]{2,1,0:T(8,128)(2,1)S(1)} %bitcast.9) | data formatting | bytes 262144
Async XLA Ops:
  57.9 1.7 %copy-start.1 = (bf16[512,128]{1,0:T(8,128)(2,1)S(1)}, bf16[512,128]{1,0:T(8,128)(2,1)}, u32[]{:S(2)}) copy-start(bf16[512,128]{1,0:T(8,128)(2,1)} %get-tuple-element.7) | copy-start | bytes 393220
  59.7 1.0 %copy-start = (bf16[512,128]{1,0:T(8,128)(2,1)S(1)}, bf16[512,128]{1,0:T(8,128)(2,1)}, u32[]{:S(2)}) copy-start(bf16[512,128]{1,0:T(8,128)(2,1)} %get-tuple-element.8) | copy-start | bytes 393220

commit v2 on v1

--- a/solution.py
+++ b/solution.py
@@ -239,17 +239,16 @@
         return gpart[kind, w * CORES + core] + sib_in[kind, w].astype(F32)
 
     def hand_down(kind, w):
-        ch_out[kind, w] = summed(kind, w).astype(BF16)
+        mine = gpart.at[kind, w * CORES + core]
+        mine[...] = summed(kind, w)
 
         @pl.when(not_top)
         def _():
             grad_down(kind, w).wait_recv()
-            ch_out[kind, w] = (summed_again(kind, w) + ch_in[kind, w].astype(F32)).astype(BF16)
-
+            mine[...] += ch_in[kind, w].astype(F32)
+
+        ch_out[kind, w] = mine[...].astype(BF16)
         grad_down(kind, w).start()
-
-    def summed_again(kind, w):
-        return gpart[kind, w * CORES + core] + sib_in[kind, w].astype(F32)
 
     @pl.when(jnp.logical_and(not_top, chip == 0))
     def _():
@@ -329,6 +328,13 @@
     @pl.loop(0, end)
     def _(t):
         w = chip + end - 1 - t
+
+        @pl.when(jnp.logical_and(not_top, w == chip))
+        def _():
+            @pl.loop(0, chip)
+            def _(s):
+                hand_down(1, chip - 1 - s)
+
         value_grads(w, True)
 
         @pl.when(w > chip)
@@ -343,12 +349,6 @@
             for kind in range(2):
                 ch_out[kind, w] = summed(kind, w).astype(BF16)
                 grad_up(kind).start()
-
-    @pl.when(not_top)
-    def _():
-        @pl.loop(0, chip)
-        def _(t):
-            hand_down(1, chip - 1 - t)
 
     for h in range(heads):
         rows = slice(h * query_rows, (h + 1) * query_rows)
@@ -410,7 +410,7 @@
     cols = query_rows * (width // HD)
     look = (SEG_MOST + key_rows - 2) // key_rows
     assert look <= CORES and ranks % CORES == 0
-    chunk = math.gcd(key_rows, 256)
+    chunk = math.gcd(key_rows, 512)
     parts = key_rows // chunk
     keep = ranks * key_rows * cols * 4 <= KEEP_BYTES
     kept = ranks if keep else 1

time: 61.4 us -> 57.7 us (0.940)
  Pallas kernels: 57.3 us -> 53.6 us
    pallas_call x1, Pallas kernels: 57.3 us -> 53.6 us  [per_device(): pl.pallas_call(functools.partial(fused, ranks, look, chunk, keep), out_sh...]
where the time goes in v2:
time: 57.7 us; the launch traced here: 57.5 us
  Pallas kernels  53.6 us (93%)
  local copies, waits for them, and re-layouts  3.31 us (6%)
  between operations  0.65 us (1%)
    pallas_call x1, Pallas kernels, per_device(): pl.pallas_call(functools.partial(fused, ranks, look, chunk, keep), out_sh...  53.6 us
    unnamed x7, local copies, waits for them, and re-layouts  3.31 us

profile of v2, /device:TPU:0, one launch (start us, length us, event | category | flops | bytes accessed | tf_op | source)
XLA Modules:
  0.0 57.5 jit_solution(11745376399905170363)
XLA Ops:
  0.6 53.6 %shard_map.94 = (bf16[128,1024]{1,0:T(8,128)(2,1)}, bf16[512,128]{1,0:T(8,128)(2,1)}, bf16[512,128]{1,0:T(8,128)(2,1)}) custom-call(bf16[128,1024]{1,0:T(8,128)(2,1)} %bitcast.11, bf16[512,128]{1,0:T(8,128)(2,1)} %bitcast.14, bf16[512,128]{1,0:T(8,128)(2,1)} %bitcast.15, bf16[128,1024]{1,0:T(8,128)(2,1)} %bitcast.12, bf16[128,1024]{1,0:T(8,128)(2,1)} %bitcast.13, ...), custom_call_target="tpu_custom_call" | custom-call | flops 6442450944 | bytes 1048576 | tf_op jit(solution)/shard_map/pallas_call | solution.py:421
  54.2 0.0 copy-start.1
  54.2 1.7 %copy.13 = bf16[1,128,1024]{2,1,0:T(8,128)(2,1)} copy(bf16[1,128,1024]{2,1,0:T(8,128)(2,1)} %bitcast.8) | data formatting | bytes 524288
  55.9 0.0 copy-done.1
  55.9 0.0 copy-start
  55.9 0.7 %copy.14 = bf16[1,512,128]{2,1,0:T(8,128)(2,1)} copy(bf16[1,512,128]{2,1,0:T(8,128)(2,1)S(1)} %bitcast.10) | data formatting | bytes 262144
  56.6 0.3 copy-done
  56.9 0.7 %copy.15 = bf16[1,512,128]{2,1,0:T(8,128)(2,1)} copy(bf16[1,512,128]{2,1,0:T(8,128)(2,1)S(1)} %bitcast.9) | data formatting | bytes 262144
Async XLA Ops:
  54.2 1.7 %copy-start.1 = (bf16[512,128]{1,0:T(8,128)(2,1)S(1)}, bf16[512,128]{1,0:T(8,128)(2,1)}, u32[]{:S(2)}) copy-start(bf16[512,128]{1,0:T(8,128)(2,1)} %get-tuple-element.7) | copy-start | bytes 393220
  55.9 1.0 %copy-start = (bf16[512,128]{1,0:T(8,128)(2,1)S(1)}, bf16[512,128]{1,0:T(8,128)(2,1)}, u32[]{:S(2)}) copy-start(bf16[512,128]{1,0:T(8,128)(2,1)} %get-tuple-element.8) | copy-start | bytes 393220

commit v3 on v2

--- a/solution.py
+++ b/solution.py
@@ -34,7 +34,7 @@
     q_ref, k_ref, v_ref, do_ref, o_ref, seg_ref, flag_ref,
     dq_ref, dk_ref, dv_ref,
     kbuf, vbuf, ebuf, tops, qcols, qrows, docols, dorows, reach, odot, top, total, lse, dqt,
-    gpart, sib_out, sib_in, ch_out, ch_in, low_in, segs,
+    low, gpart, sib_out, sib_in, ch_out, ch_in, low_in, segs,
     k_up, k_side, k_down, k_recv, v_up, v_side, v_down, v_recv,
     gs_send, gs_recv, gc_send, gc_recv, gl_send, gl_recv, seg_send, seg_recv,
 ):
@@ -44,6 +44,8 @@
     heads = q_ref.shape[1] // HD
     cols = query_rows * heads
     parts = key_rows // chunk
+    strip = math.gcd(cols, 256)
+    piece = math.gcd(chunk, 64)
     scale = 1.0 / math.sqrt(HD)
     factor = scale * math.log2(math.e)
     me = lax.axis_index("ctx")
@@ -146,8 +148,8 @@
     for d in range(look + 1):
         for j in range(key_rows // HD):
             at = slice(j * HD, (j + 1) * HD)
-            piece = (seg_ref[:, at] if d == 0 else segs[d - 1, :, at]).astype(F32)
-            counts = counts + jnp.where(piece <= seg_col, 1.0, 0.0)
+            ids_row = (seg_ref[:, at] if d == 0 else segs[d - 1, :, at]).astype(F32)
+            counts = counts + jnp.where(ids_row <= seg_col, 1.0, 0.0)
     count = jnp.sum(counts, axis=1, keepdims=True)
     segments = flag_ref.shape[1]
     ids = lax.broadcasted_iota(jnp.int32, (query_rows, segments), 1).astype(F32)
@@ -162,28 +164,39 @@
     def rows_of(part):
         return pl.ds(pl.multiple_of(part * chunk, chunk), chunk)
 
-    def scores_of(slot, part, masked):
-        s = jnp.dot(kbuf[slot, rows_of(part), :], qcols[...], preferred_element_type=F32) * factor
+    def masked_scores(slot, part, at, masked):
+        s = jnp.dot(kbuf[slot, rows_of(part), :], qcols[:, at], preferred_element_type=F32)
         if masked:
             first = slot * key_rows + part * chunk
-            pos = first + lax.broadcasted_iota(jnp.int32, (chunk, cols), 0)
-            s = jnp.where(pos <= reach[...], s, LOW)
+            pos = first + lax.broadcasted_iota(jnp.int32, s.shape, 0)
+            s = jnp.where(pos <= reach[:, at], s, LOW)
         return s
+
+    strips = [slice(i, i + strip) for i in range(0, cols, strip)]
+    slices = [slice(i, i + piece) for i in range(0, chunk, piece)]
+
+    def slice_of(part, rows):
+        return pl.ds(pl.multiple_of(part * chunk + rows.start, piece), piece)
 
     def stats(slot, masked):
         @pl.loop(0, parts)
         def _(part):
-            s = scores_of(slot, part, masked)
-            here = jnp.maximum(jnp.max(s, axis=0, keepdims=True), FLOOR)
-            e = jnp.exp2(s - here)
-            if keep:
-                ebuf[slot, rows_of(part), :] = e
-                tops[slot * parts + part] = here
-            old = top[...]
-            new = jnp.maximum(old, here)
-            total[...] = total[...] * jnp.exp2(old - new) + (
-                jnp.sum(e, axis=0, keepdims=True) * jnp.exp2(here - new))
-            top[...] = new
+            for at in strips:
+                s = masked_scores(slot, part, at, masked)
+                here = jnp.maximum(jnp.max(s, axis=0, keepdims=True), FLOOR)
+                added = jnp.zeros((1, strip), F32)
+                for rows in slices:
+                    e = jnp.exp2((s[rows] - here) * factor)
+                    if keep:
+                        ebuf[slot, slice_of(part, rows), at] = e
+                    added = added + jnp.sum(e, axis=0, keepdims=True)
+                here = here * factor
+                if keep:
+                    tops[slot * parts + part, :, at] = here
+                old = top[:, at]
+                new = jnp.maximum(old, here)
+                total[:, at] = total[:, at] * jnp.exp2(old - new) + added * jnp.exp2(here - new)
+                top[:, at] = new
 
     def chip_stats(w, masked):
         @pl.loop(0, CORES)
@@ -196,10 +209,12 @@
 
             stats(slot, masked)
 
-    def probs_of(slot, part, masked):
+    def probs_of(slot, part, at, masked):
         if keep:
-            return ebuf[slot, rows_of(part), :] * jnp.exp2(tops[slot * parts + part] - lse[...])
-        return jnp.exp2(scores_of(slot, part, masked) - lse[...])
+            level = jnp.exp2(tops[slot * parts + part, :, at] - lse[:, at])
+            return lambda rows: ebuf[slot, slice_of(part, rows), at] * level
+        s = masked_scores(slot, part, at, masked)
+        return lambda rows: jnp.exp2(s[rows] * factor - lse[:, at])
 
     def send_side(kind, w):
         sib_out[kind, w] = gpart[kind, w * CORES + (1 - core)].astype(BF16)
@@ -210,8 +225,11 @@
         def _(i):
             slot = w * CORES + i // parts
             part = i % parts
-            p = probs_of(slot, part, masked).astype(BF16)
-            gpart[0, slot, rows_of(part), :] = jnp.dot(p, dorows[...], preferred_element_type=F32)
+            for at in strips:
+                probs = probs_of(slot, part, at, masked)
+                for rows in slices:
+                    low[rows, at] = probs(rows).astype(BF16)
+            gpart[0, slot, rows_of(part), :] = jnp.dot(low[...], dorows[...], preferred_element_type=F32)
 
         send_side(0, w)
 
@@ -226,11 +244,14 @@
 
             @pl.loop(0, parts)
             def _(part):
-                p = probs_of(slot, part, masked)
-                dp = jnp.dot(vbuf[slot, rows_of(part), :], docols[...], preferred_element_type=F32)
-                ds = (p * (dp - odot[...])).astype(BF16)
-                gpart[1, slot, rows_of(part), :] = scale * jnp.dot(ds, qrows[...], preferred_element_type=F32)
-                dqt[...] += jnp.dot(kbuf[slot, rows_of(part), :].T, ds, preferred_element_type=F32)
+                keys_t = kbuf[slot, rows_of(part), :].T
+                for at in strips:
+                    probs = probs_of(slot, part, at, masked)
+                    dp = jnp.dot(vbuf[slot, rows_of(part), :], docols[:, at], preferred_element_type=F32)
+                    for rows in slices:
+                        low[rows, at] = (probs(rows) * (dp[rows] - odot[:, at])).astype(BF16)
+                    dqt[:, at] += jnp.dot(keys_t, low[:, at], preferred_element_type=F32)
+                gpart[1, slot, rows_of(part), :] = scale * jnp.dot(low[...], qrows[...], preferred_element_type=F32)
 
         send_side(1, w)
 
@@ -442,6 +463,7 @@
             pltpu.VMEM((1, cols), F32),
             pltpu.VMEM((1, cols), F32),
             pltpu.VMEM((HD, cols), F32),
+            pltpu.VMEM((chunk, cols), BF16),
             pltpu.VMEM((2, ranks) + block, F32),
             pltpu.VMEM(grads, BF16),
             pltpu.VMEM(grads, BF16),

time: 57.7 us -> 59.1 us (1.024)
  Pallas kernels: 53.6 us -> 54.9 us
    pallas_call x1, Pallas kernels: 53.6 us -> 54.9 us  [per_device(): pl.pallas_call(functools.partial(fused, ranks, look, chunk, keep), out_sh...]
where the time goes in v3:
time: 59.1 us; the launch traced here: 58.9 us
  Pallas kernels  54.9 us (93%)
  local copies, waits for them, and re-layouts  3.31 us (6%)
  between operations  0.65 us (1%)
    pallas_call x1, Pallas kernels, per_device(): pl.pallas_call(functools.partial(fused, ranks, look, chunk, keep), out_sh...  54.9 us
    unnamed x7, local copies, waits for them, and re-layouts  3.31 us

profile of v3, /device:TPU:0, one launch (start us, length us, event | category | flops | bytes accessed | tf_op | source)
XLA Modules:
  0.0 58.9 jit_solution(4129035332328786409)
XLA Ops:
  0.6 54.9 %shard_map.94 = (bf16[128,1024]{1,0:T(8,128)(2,1)}, bf16[512,128]{1,0:T(8,128)(2,1)}, bf16[512,128]{1,0:T(8,128)(2,1)}) custom-call(bf16[128,1024]{1,0:T(8,128)(2,1)} %bitcast.11, bf16[512,128]{1,0:T(8,128)(2,1)} %bitcast.14, bf16[512,128]{1,0:T(8,128)(2,1)} %bitcast.15, bf16[128,1024]{1,0:T(8,128)(2,1)} %bitcast.12, bf16[128,1024]{1,0:T(8,128)(2,1)} %bitcast.13, ...), custom_call_target="tpu_custom_call" | custom-call | flops 6442450944 | bytes 1048576 | tf_op jit(solution)/shard_map/pallas_call | solution.py:442
  55.6 0.0 copy-start.1
  55.6 1.7 %copy.13 = bf16[1,128,1024]{2,1,0:T(8,128)(2,1)} copy(bf16[1,128,1024]{2,1,0:T(8,128)(2,1)} %bitcast.8) | data formatting | bytes 524288
  57.3 0.0 copy-done.1
  57.3 0.0 copy-start
  57.3 0.7 %copy.14 = bf16[1,512,128]{2,1,0:T(8,128)(2,1)} copy(bf16[1,512,128]{2,1,0:T(8,128)(2,1)S(1)} %bitcast.10) | data formatting | bytes 262144
  57.9 0.3 copy-done
  58.2 0.7 %copy.15 = bf16[1,512,128]{2,1,0:T(8,128)(2,1)} copy(bf16[1,512,128]{2,1,0:T(8,128)(2,1)S(1)} %bitcast.9) | data formatting | bytes 262144
Async XLA Ops:
  55.6 1.7 %copy-start.1 = (bf16[512,128]{1,0:T(8,128)(2,1)S(1)}, bf16[512,128]{1,0:T(8,128)(2,1)}, u32[]{:S(2)}) copy-start(bf16[512,128]{1,0:T(8,128)(2,1)} %get-tuple-element.7) | copy-start | bytes 393220
  57.3 1.0 %copy-start = (bf16[512,128]{1,0:T(8,128)(2,1)S(1)}, bf16[512,128]{1,0:T(8,128)(2,1)}, u32[]{:S(2)}) copy-start(bf16[512,128]{1,0:T(8,128)(2,1)} %get-tuple-element.8) | copy-start | bytes 393220

commit v4 on v2

--- a/solution.py
+++ b/solution.py
@@ -11,6 +11,7 @@
 HD = 128
 SEG_MOST = 1024
 CORES = 2
+HALVES = 2
 LOW = -1e30
 FLOOR = -1e29
 KEEP_BYTES = 20 * 1024 * 1024
@@ -35,7 +36,7 @@
     dq_ref, dk_ref, dv_ref,
     kbuf, vbuf, ebuf, tops, qcols, qrows, docols, dorows, reach, odot, top, total, lse, dqt,
     gpart, sib_out, sib_in, ch_out, ch_in, low_in, segs,
-    k_up, k_side, k_down, k_recv, v_up, v_side, v_down, v_recv,
+    k_up, k_low, k_side, k_down, k_recv, v_up, v_low, v_side, v_down, v_recv,
     gs_send, gs_recv, gc_send, gc_recv, gl_send, gl_recv, seg_send, seg_recv,
 ):
     chips = ranks // CORES
@@ -74,9 +75,20 @@
     vbuf[own_slot] = v_ref[...]
     pl.semaphore_wait(barrier, there)
 
-    def up(buf, sems, recv, w):
-        slot = w * CORES + core
-        return push(buf.at[slot], buf.at[slot], sems.at[w], recv.at[slot], me + CORES)
+    def up(buf, sems, recv, w, half, rank):
+        rows = pl.ds(half * (key_rows // HALVES), key_rows // HALVES)
+        place = buf.at[w * CORES + core, rows]
+        return push(place, place, sems.at[w, half], recv.at[w, half], rank)
+
+    def start_up(buf, sems, recv, w):
+        for half in range(HALVES):
+            up(buf, sems, recv, w, half, me + CORES).start()
+
+    def from_below(buf, sems, recv, w, forward):
+        for half in range(HALVES):
+            up(buf, sems, recv, w, half, side).wait_recv()
+            if forward:
+                up(buf, sems, recv, w, half, me + CORES).start()
 
     def across(buf, sems, recv, w):
         slot = w * CORES + core
@@ -102,7 +114,7 @@
 
     @pl.when(not_top)
     def _():
-        up(kbuf, k_up, k_recv, chip).start()
+        start_up(kbuf, k_up, k_low, chip)
 
     across(kbuf, k_side, k_recv, chip).start()
     for d in range(1, look + 1):
@@ -250,26 +262,25 @@
         ch_out[kind, w] = mine[...].astype(BF16)
         grad_down(kind, w).start()
 
-    @pl.when(jnp.logical_and(not_top, chip == 0))
-    def _():
-        up(vbuf, v_up, v_recv, chip).start()
+    @pl.when(not_top)
+    def _():
+        @pl.loop(1, chip + 1)
+        def _(s):
+            from_below(kbuf, k_up, k_low, chip - s, True)
+            across(kbuf, k_side, k_recv, chip - s).start()
+
+        start_up(vbuf, v_up, v_low, chip)
 
     chip_stats(chip, True)
 
     @pl.loop(1, chip + 1)
     def _(s):
         w = chip - s
-        arrived(kbuf, k_side, k_recv, w * CORES + core)
-
-        @pl.when(not_top)
-        def _():
-            up(kbuf, k_up, k_recv, w).start()
-
-        across(kbuf, k_side, k_recv, w).start()
-
-        @pl.when(jnp.logical_and(not_top, w == 0))
-        def _():
-            up(vbuf, v_up, v_recv, chip).start()
+
+        @pl.when(is_top)
+        def _():
+            from_below(kbuf, k_up, k_low, w, False)
+            across(kbuf, k_side, k_recv, w).start()
 
         chip_stats(w, False)
 
@@ -288,8 +299,7 @@
 
         @pl.when(not_top)
         def _():
-            arrived(vbuf, v_side, v_recv, w * CORES + core)
-            up(vbuf, v_up, v_recv, w).start()
+            from_below(vbuf, v_up, v_low, w, True)
             across(vbuf, v_side, v_recv, w).start()
 
         @pl.when(jnp.logical_and(is_top, t > 0))
@@ -306,22 +316,12 @@
 
         @pl.when(is_top)
         def _():
-            arrived(vbuf, v_side, v_recv, w * CORES + core)
+            from_below(vbuf, v_up, v_low, w, False)
             across(vbuf, v_side, v_recv, w).start()
 
         key_grads(w, False)
 
-        @pl.when(jnp.logical_and(is_top, t > 0))
-        def _():
-            hand_down(1, w + 1)
-
-        @pl.when(not_top)
-        def _():
-            hand_down(0, w)
-
-    @pl.when(jnp.logical_and(is_top, has_low))
-    def _():
-        hand_down(1, 0)
+        hand_down(jnp.where(is_top, 1, 0), w)
 
     end = jnp.where(not_top, 2, 1)
 
@@ -393,13 +393,20 @@
 
         @pl.when(jnp.logical_and(not_top, w <= chip))
         def _():
-            up(kbuf, k_up, k_recv, w).wait_send()
-            up(vbuf, v_up, v_recv, w).wait_send()
+            for half in range(HALVES):
+                up(kbuf, k_up, k_low, w, half, side).wait_send()
+                up(vbuf, v_up, v_low, w, half, side).wait_send()
 
         @pl.when(w < chip)
         def _():
             for kind in range(2):
                 grad_down(kind, w).wait_send()
+
+
+def pass_on(a_ref, b_ref, c_ref, a_out, b_out, c_out):
+    a_out[...] = a_ref[...]
+    b_out[...] = b_ref[...]
+    c_out[...] = c_ref[...]
 
 
 def per_device(queries, keys, values, grad_out, saved_out, segment_ids, frame_flags):
@@ -449,8 +456,8 @@
             pltpu.VMEM(grads, BF16),
             pltpu.VMEM((2,) + block, BF16),
             pltpu.VMEM((look, 1, key_rows), jnp.int32),
-            dma((chips,)), dma((chips,)), dma((1,)), dma((ranks,)),
-            dma((chips,)), dma((chips,)), dma((1,)), dma((ranks,)),
+            dma((chips, HALVES)), dma((chips, HALVES)), dma((chips,)), dma((1,)), dma((ranks,)),
+            dma((chips, HALVES)), dma((chips, HALVES)), dma((chips,)), dma((1,)), dma((ranks,)),
             dma((2, chips)), dma((2, chips)), dma((2, chips)), dma((2, chips)),
             dma((2,)), dma((2,)), dma((look,)), dma((look,)),
         ],
@@ -463,7 +470,13 @@
             transcendentals=cols * ranks * key_rows,
         ),
     )(queries[0], keys[0], values[0], grad_out[0], saved_out[0], segment_ids, frame_flags)
-    return grad_queries[None], grad_keys[None], grad_values[None]
+    results = pl.pallas_call(
+        pass_on,
+        out_shape=tuple(jax.ShapeDtypeStruct(r.shape, r.dtype) for r in (grad_queries, grad_keys, grad_values)),
+        in_specs=[vmem] * 3,
+        out_specs=(vmem,) * 3,
+    )(grad_queries, grad_keys, grad_values)
+    return tuple(r[None] for r in results)
 
 
 def solution(mesh):

time: 57.7 us -> 53.5 us (0.927)
  local copies, waits for them, and re-layouts: 3.31 us -> 0 us
  Pallas kernels: 53.6 us -> 52.7 us
    unnamed x7 -> x0, local copies, waits for them, and re-layouts: 3.31 us -> none
    pallas_call x1, Pallas kernels: 53.6 us -> 50.9 us  [per_device(): pl.pallas_call(functools.partial(fused, ranks, look, chunk, keep), out_sh...]
    pallas_call x0 -> x1, Pallas kernels: none -> 1.84 us  [per_device(): pl.pallas_call(pass_on, out_shape=tuple((jax.ShapeDtypeStruct(r.shape, r....]
where the time goes in v4:
time: 53.5 us; the launch traced here: 53.3 us
  Pallas kernels  52.7 us (99%)
  between operations  0.64 us (1%)
    pallas_call x1, Pallas kernels, per_device(): pl.pallas_call(functools.partial(fused, ranks, look, chunk, keep), out_sh...  50.9 us
    pallas_call x1, Pallas kernels, per_device(): pl.pallas_call(pass_on, out_shape=tuple((jax.ShapeDtypeStruct(r.shape, r....  1.84 us

profile of v4, /device:TPU:0, one launch (start us, length us, event | category | flops | bytes accessed | tf_op | source)
XLA Modules:
  0.0 53.3 jit_solution(2263864348607120563)
XLA Ops:
  0.6 50.9 %shard_map.94 = (bf16[128,1024]{1,0:T(8,128)(2,1)}, bf16[512,128]{1,0:T(8,128)(2,1)}, bf16[512,128]{1,0:T(8,128)(2,1)}) custom-call(bf16[128,1024]{1,0:T(8,128)(2,1)} %bitcast.8, bf16[512,128]{1,0:T(8,128)(2,1)} %bitcast.12, bf16[512,128]{1,0:T(8,128)(2,1)} %bitcast.13, bf16[128,1024]{1,0:T(8,128)(2,1)} %bitcast.9, bf16[128,1024]{1,0:T(8,128)(2,1)} %bitcast.10, ...), custom_call_target="tpu_custom_call" | custom-call | flops 6442450944 | bytes 1048576 | tf_op jit(solution)/shard_map/pallas_call | solution.py:428
  51.5 1.8 %shard_map.95 = (bf16[128,1024]{1,0:T(8,128)(2,1)}, bf16[512,128]{1,0:T(8,128)(2,1)}, bf16[512,128]{1,0:T(8,128)(2,1)}) custom-call(bf16[128,1024]{1,0:T(8,128)(2,1)} %get-tuple-element.9.a_ref, bf16[512,128]{1,0:T(8,128)(2,1)} %get-tuple-element.10.b_ref, bf16[512,128]{1,0:T(8,128)(2,1)} %get-tuple-element.11.c_ref), custom_call_target="tpu_custom_call" | custom-call | tf_op jit(solution)/shard_map/pallas_call | solution.py:473

commit v5 on v4

--- a/solution.py
+++ b/solution.py
@@ -178,8 +178,8 @@
         s = jnp.dot(kbuf[slot, rows_of(part), :], qcols[...], preferred_element_type=F32) * factor
         if masked:
             first = slot * key_rows + part * chunk
-            pos = first + lax.broadcasted_iota(jnp.int32, (chunk, cols), 0)
-            s = jnp.where(pos <= reach[...], s, LOW)
+            pos = lax.broadcasted_iota(jnp.int32, (chunk, cols), 0)
+            s = jnp.where(pos <= reach[...] - first, s, LOW)
         return s
 
     def stats(slot, masked):
@@ -189,7 +189,7 @@
             here = jnp.maximum(jnp.max(s, axis=0, keepdims=True), FLOOR)
             e = jnp.exp2(s - here)
             if keep:
-                ebuf[slot, rows_of(part), :] = e
+                ebuf[slot, rows_of(part), :] = e.astype(BF16)
                 tops[slot * parts + part] = here
             old = top[...]
             new = jnp.maximum(old, here)
@@ -210,7 +210,8 @@
 
     def probs_of(slot, part, masked):
         if keep:
-            return ebuf[slot, rows_of(part), :] * jnp.exp2(tops[slot * parts + part] - lse[...])
+            level = jnp.exp2(tops[slot * parts + part] - lse[...])
+            return ebuf[slot, rows_of(part), :].astype(F32) * level
         return jnp.exp2(scores_of(slot, part, masked) - lse[...])
 
     def send_side(kind, w):
@@ -223,6 +224,8 @@
             slot = w * CORES + i // parts
             part = i % parts
             p = probs_of(slot, part, masked).astype(BF16)
+            if keep:
+                ebuf[slot, rows_of(part), :] = p
             gpart[0, slot, rows_of(part), :] = jnp.dot(p, dorows[...], preferred_element_type=F32)
 
         send_side(0, w)
@@ -238,7 +241,7 @@
 
             @pl.loop(0, parts)
             def _(part):
-                p = probs_of(slot, part, masked)
+                p = ebuf[slot, rows_of(part), :].astype(F32) if keep else probs_of(slot, part, masked)
                 dp = jnp.dot(vbuf[slot, rows_of(part), :], docols[...], preferred_element_type=F32)
                 ds = (p * (dp - odot[...])).astype(BF16)
                 gpart[1, slot, rows_of(part), :] = scale * jnp.dot(ds, qrows[...], preferred_element_type=F32)
@@ -403,10 +406,13 @@
                 grad_down(kind, w).wait_send()
 
 
-def pass_on(a_ref, b_ref, c_ref, a_out, b_out, c_out):
-    a_out[...] = a_ref[...]
-    b_out[...] = b_ref[...]
-    c_out[...] = c_ref[...]
+def pass_on(a_ref, b_ref, c_ref, a_out, b_out, c_out, sems):
+    pairs = ((a_ref, a_out), (b_ref, b_out), (c_ref, c_out))
+    copies = [pltpu.make_async_copy(src, dst, sems.at[i]) for i, (src, dst) in enumerate(pairs)]
+    for copy in copies:
+        copy.start()
+    for copy in copies:
+        copy.wait()
 
 
 def per_device(queries, keys, values, grad_out, saved_out, segment_ids, frame_flags):
@@ -437,7 +443,7 @@
         scratch_shapes=[
             pltpu.VMEM((ranks,) + block, BF16),
             pltpu.VMEM((ranks,) + block, BF16),
-            pltpu.VMEM((kept, key_rows, cols), F32) if keep else pltpu.VMEM((8, 128), F32),
+            pltpu.VMEM((kept, key_rows, cols), BF16) if keep else pltpu.VMEM((8, 128), F32),
             pltpu.VMEM((kept * parts, 1, cols), F32),
             pltpu.VMEM((HD, cols), BF16),
             pltpu.VMEM((cols, HD), BF16),
@@ -473,8 +479,9 @@
     results = pl.pallas_call(
         pass_on,
         out_shape=tuple(jax.ShapeDtypeStruct(r.shape, r.dtype) for r in (grad_queries, grad_keys, grad_values)),
-        in_specs=[vmem] * 3,
-        out_specs=(vmem,) * 3,
+        in_specs=[pl.BlockSpec(memory_space=pl.ANY)] * 3,
+        out_specs=(pl.BlockSpec(memory_space=pl.ANY),) * 3,
+        scratch_shapes=[dma((3,))],
     )(grad_queries, grad_keys, grad_values)
     return tuple(r[None] for r in results)
 

time: 53.5 us -> 68.7 us (1.28)
  Pallas kernels: 52.7 us -> 67.9 us
    pallas_call x1, Pallas kernels: 1.84 us -> 17 us  [per_device(): pl.pallas_call(pass_on, out_shape=tuple((jax.ShapeDtypeStruct(r.shape, r....]
where the time goes in v5:
time: 68.7 us; the launch traced here: 68.5 us
  Pallas kernels  67.9 us (99%)
    pallas_call x1, Pallas kernels, per_device(): pl.pallas_call(functools.partial(fused, ranks, look, chunk, keep), out_sh...  50.9 us
    pallas_call x1, Pallas kernels, per_device(): pl.pallas_call(pass_on, out_shape=tuple((jax.ShapeDtypeStruct(r.shape, r....  17 us

profile of v5, /device:TPU:0, one launch (start us, length us, event | category | flops | bytes accessed | tf_op | source)
XLA Modules:
  0.0 68.5 jit_solution(17509548802526480698)
XLA Ops:
  0.6 50.9 %shard_map.94 = (bf16[128,1024]{1,0:T(8,128)(2,1)}, bf16[512,128]{1,0:T(8,128)(2,1)}, bf16[512,128]{1,0:T(8,128)(2,1)}) custom-call(bf16[128,1024]{1,0:T(8,128)(2,1)} %bitcast.8, bf16[512,128]{1,0:T(8,128)(2,1)} %bitcast.12, bf16[512,128]{1,0:T(8,128)(2,1)} %bitcast.13, bf16[128,1024]{1,0:T(8,128)(2,1)} %bitcast.9, bf16[128,1024]{1,0:T(8,128)(2,1)} %bitcast.10, ...), custom_call_target="tpu_custom_call" | custom-call | flops 6442450944 | bytes 1048576 | tf_op jit(solution)/shard_map/pallas_call | solution.py:434
  51.5 17.0 %shard_map.95 = (bf16[128,1024]{1,0:T(8,128)(2,1)}, bf16[512,128]{1,0:T(8,128)(2,1)}, bf16[512,128]{1,0:T(8,128)(2,1)}) custom-call(bf16[128,1024]{1,0:T(8,128)(2,1)} %get-tuple-element.9.a_ref, bf16[512,128]{1,0:T(8,128)(2,1)} %get-tuple-element.10.b_ref, bf16[512,128]{1,0:T(8,128)(2,1)} %get-tuple-element.11.c_ref), custom_call_target="tpu_custom_call" | custom-call | tf_op jit(solution)/shard_map/pallas_call | solution.py:479

commit v6 on v4

--- a/solution.py
+++ b/solution.py
@@ -106,8 +106,13 @@
     def grad_side(kind, w):
         return push(sib_out.at[kind, w], sib_in.at[kind, w], gs_send.at[kind, w], gs_recv.at[kind, w], side)
 
-    def grad_down(kind, w):
-        return push(ch_out.at[kind, w], ch_in.at[kind, w], gc_send.at[kind, w], gc_recv.at[kind, w], me - CORES)
+    def half_of(half):
+        return pl.ds(half * (key_rows // HALVES), key_rows // HALVES)
+
+    def grad_down(kind, w, half, rank):
+        rows = half_of(half)
+        return push(ch_out.at[kind, w, rows], ch_in.at[kind, w, rows],
+                    gc_send.at[kind, w, half], gc_recv.at[kind, w, half], rank)
 
     def grad_up(kind):
         return push(ch_out.at[kind, chip + 1], low_in.at[kind], gl_send.at[kind], gl_recv.at[kind], me + CORES)
@@ -253,14 +258,16 @@
     def hand_down(kind, w):
         mine = gpart.at[kind, w * CORES + core]
         mine[...] = summed(kind, w)
-
-        @pl.when(not_top)
-        def _():
-            grad_down(kind, w).wait_recv()
-            mine[...] += ch_in[kind, w].astype(F32)
-
-        ch_out[kind, w] = mine[...].astype(BF16)
-        grad_down(kind, w).start()
+        for half in range(HALVES):
+            rows = half_of(half)
+
+            @pl.when(not_top)
+            def _():
+                grad_down(kind, w, half, side).wait_recv()
+                mine[rows, :] += ch_in[kind, w, rows, :].astype(F32)
+
+            ch_out[kind, w, rows, :] = mine[rows, :].astype(BF16)
+            grad_down(kind, w, half, me - CORES).start()
 
     @pl.when(not_top)
     def _():
@@ -364,7 +371,8 @@
 
         @pl.when(not_top)
         def _():
-            grad_down(kind, chip).wait_recv()
+            for half in range(HALVES):
+                grad_down(kind, chip, half, side).wait_recv()
             gpart[kind, own_slot] = gpart[kind, own_slot] + ch_in[kind, chip].astype(F32)
 
         out[...] = gpart[kind, own_slot].astype(BF16)
@@ -400,7 +408,8 @@
         @pl.when(w < chip)
         def _():
             for kind in range(2):
-                grad_down(kind, w).wait_send()
+                for half in range(HALVES):
+                    grad_down(kind, w, half, side).wait_send()
 
 
 def pass_on(a_ref, b_ref, c_ref, a_out, b_out, c_out):
@@ -458,7 +467,7 @@
             pltpu.VMEM((look, 1, key_rows), jnp.int32),
             dma((chips, HALVES)), dma((chips, HALVES)), dma((chips,)), dma((1,)), dma((ranks,)),
             dma((chips, HALVES)), dma((chips, HALVES)), dma((chips,)), dma((1,)), dma((ranks,)),
-            dma((2, chips)), dma((2, chips)), dma((2, chips)), dma((2, chips)),
+            dma((2, chips)), dma((2, chips)), dma((2, chips, HALVES)), dma((2, chips, HALVES)),
             dma((2,)), dma((2,)), dma((look,)), dma((look,)),
         ],
         compiler_params=pltpu.CompilerParams(

time: 53.5 us -> 52.1 us (0.974)
  Pallas kernels: 52.7 us -> 51.3 us
    pallas_call x1, Pallas kernels: 50.9 us -> 49.4 us  [per_device(): pl.pallas_call(functools.partial(fused, ranks, look, chunk, keep), out_sh...]
where the time goes in v6:
time: 52.1 us; the launch traced here: 51.9 us
  Pallas kernels  51.3 us (98%)
  between operations  0.64 us (1%)
    pallas_call x1, Pallas kernels, per_device(): pl.pallas_call(functools.partial(fused, ranks, look, chunk, keep), out_sh...  49.4 us
    pallas_call x1, Pallas kernels, per_device(): pl.pallas_call(pass_on, out_shape=tuple((jax.ShapeDtypeStruct(r.shape, r....  1.84 us

profile of v6, /device:TPU:0, one launch (start us, length us, event | category | flops | bytes accessed | tf_op | source)
XLA Modules:
  0.0 51.9 jit_solution(7899270641019934742)
XLA Ops:
  0.6 49.4 %shard_map.94 = (bf16[128,1024]{1,0:T(8,128)(2,1)}, bf16[512,128]{1,0:T(8,128)(2,1)}, bf16[512,128]{1,0:T(8,128)(2,1)}) custom-call(bf16[128,1024]{1,0:T(8,128)(2,1)} %bitcast.8, bf16[512,128]{1,0:T(8,128)(2,1)} %bitcast.12, bf16[512,128]{1,0:T(8,128)(2,1)} %bitcast.13, bf16[128,1024]{1,0:T(8,128)(2,1)} %bitcast.9, bf16[128,1024]{1,0:T(8,128)(2,1)} %bitcast.10, ...), custom_call_target="tpu_custom_call" | custom-call | flops 6442450944 | bytes 1048576 | tf_op jit(solution)/shard_map/pallas_call | solution.py:437
  50.1 1.8 %shard_map.95 = (bf16[128,1024]{1,0:T(8,128)(2,1)}, bf16[512,128]{1,0:T(8,128)(2,1)}, bf16[512,128]{1,0:T(8,128)(2,1)}) custom-call(bf16[128,1024]{1,0:T(8,128)(2,1)} %get-tuple-element.9.a_ref, bf16[512,128]{1,0:T(8,128)(2,1)} %get-tuple-element.10.b_ref, bf16[512,128]{1,0:T(8,128)(2,1)} %get-tuple-element.11.c_ref), custom_call_target="tpu_custom_call" | custom-call | tf_op jit(solution)/shard_map/pallas_call | solution.py:482

commit v7 on v6

--- a/solution.py
+++ b/solution.py
@@ -319,7 +319,7 @@
 
     @pl.loop(0, chip)
     def _(t):
-        w = chip - 1 - t
+        w = t
 
         @pl.when(is_top)
         def _():
@@ -328,7 +328,7 @@
 
         key_grads(w, False)
 
-        hand_down(jnp.where(is_top, 1, 0), w)
+        hand_down(jnp.where(is_top, 1, 0), jnp.where(is_top, w, chip - 1 - t))
 
     end = jnp.where(not_top, 2, 1)
 
@@ -340,7 +340,7 @@
         def _():
             @pl.loop(0, chip)
             def _(s):
-                hand_down(1, chip - 1 - s)
+                hand_down(1, s)
 
         value_grads(w, True)
 

time: 52.1 us -> 49.2 us (0.944)
  Pallas kernels: 51.3 us -> 48.4 us
    pallas_call x1, Pallas kernels: 49.4 us -> 46.6 us  [per_device(): pl.pallas_call(functools.partial(fused, ranks, look, chunk, keep), out_sh...]
where the time goes in v7:
time: 49.2 us; the launch traced here: 49.1 us
  Pallas kernels  48.4 us (98%)
  between operations  0.64 us (1%)
    pallas_call x1, Pallas kernels, per_device(): pl.pallas_call(functools.partial(fused, ranks, look, chunk, keep), out_sh...  46.6 us
    pallas_call x1, Pallas kernels, per_device(): pl.pallas_call(pass_on, out_shape=tuple((jax.ShapeDtypeStruct(r.shape, r....  1.84 us

profile of v7, /device:TPU:0, one launch (start us, length us, event | category | flops | bytes accessed | tf_op | source)
XLA Modules:
  0.0 49.1 jit_solution(5014040818957397903)
XLA Ops:
  0.6 46.6 %shard_map.94 = (bf16[128,1024]{1,0:T(8,128)(2,1)}, bf16[512,128]{1,0:T(8,128)(2,1)}, bf16[512,128]{1,0:T(8,128)(2,1)}) custom-call(bf16[128,1024]{1,0:T(8,128)(2,1)} %bitcast.8, bf16[512,128]{1,0:T(8,128)(2,1)} %bitcast.12, bf16[512,128]{1,0:T(8,128)(2,1)} %bitcast.13, bf16[128,1024]{1,0:T(8,128)(2,1)} %bitcast.9, bf16[128,1024]{1,0:T(8,128)(2,1)} %bitcast.10, ...), custom_call_target="tpu_custom_call" | custom-call | flops 6442450944 | bytes 1048576 | tf_op jit(solution)/shard_map/pallas_call | solution.py:437
  47.2 1.8 %shard_map.95 = (bf16[128,1024]{1,0:T(8,128)(2,1)}, bf16[512,128]{1,0:T(8,128)(2,1)}, bf16[512,128]{1,0:T(8,128)(2,1)}) custom-call(bf16[128,1024]{1,0:T(8,128)(2,1)} %get-tuple-element.9.a_ref, bf16[512,128]{1,0:T(8,128)(2,1)} %get-tuple-element.10.b_ref, bf16[512,128]{1,0:T(8,128)(2,1)} %get-tuple-element.11.c_ref), custom_call_target="tpu_custom_call" | custom-call | tf_op jit(solution)/shard_map/pallas_call | solution.py:482
